TPU v7x, 128 devices: a whole 4x4x4 slice. The times are simulated.
128 devices in a mesh: tile: 32 (over z, x, core), group: 4 (over y).
Axes of the slice: x: 4, y: 4, z: 4, core: 2. Of those that a mesh axis runs over, the one named last changes fastest.
Arguments:
- features: bfloat16 [4, 2048, 32, 256], P('group', 'tile'), may hold values from -6 to 6
- out_grad: bfloat16 [4, 704, 14, 14, 256], P('group', 'tile'), may hold values from -6 to 6
- pair_count: int32 [4, 32, 32], P('group'), may hold values from 0 to 2, as said below
- sample_grid: int32 [4, 32, 32, 2, 4, 14], P('group', 'tile'), may hold values from 0 to 62, as said below
- first_kernel: bfloat16 [3, 3, 256, 256], replicated, may hold values from -0.125 to 0.125
- second_kernel: bfloat16 [3, 3, 256, 256], replicated, may hold values from -0.125 to 0.125
Outputs:
- feature_grad: bfloat16 [4, 2048, 32, 256], P('group', 'tile')
- first_grad: float32 [3, 3, 256, 256], replicated
- second_grad: float32 [3, 3, 256, 256], replicated
Inputs may be any that keep to these rules, and one draw needn't show every extreme that they name: Every entry is at most 2; in every scene each reader t has pair_count entries summing to exactly 22 over the owners, and every reader has some owner sending it exactly 2 regions. `sample_grid`: lower row indices are at most 62 and lower column indices at most 30; fractions lie in 0 to 15; along a slot's samples the positions (16 * lower index + fraction) ascend with a constant step of 8 to 64.
All inputs are finite; a program needn't handle non-finite values.
Results may differ from a plain program's by a relative error of at most 0.015.
Values may be sent and summed in bfloat16 or wider, within the bound.
A program may use at most 256 MiB of HBM per device.

v0:
```python
import math

import jax
import jax.numpy as jnp
from jax import lax
from jax.sharding import PartitionSpec as P


def interp_weights(lower_index, fraction, extent):
    places = jnp.arange(extent, dtype=jnp.int32)
    upper_share = fraction.astype(jnp.float32) / 16.0
    lower_part = jnp.where(places == lower_index[..., None], 1.0 - upper_share[..., None], 0.0)
    upper_part = jnp.where(places == lower_index[..., None] + 1, upper_share[..., None], 0.0)
    return lower_part + upper_part


def column_weights(slot_grid, across):
    return interp_weights(slot_grid[..., 2, :], slot_grid[..., 3, :], across).astype(jnp.bfloat16)


def sample_blocks(tile_image, lower_rows, lower_weight, upper_weight, col_weights):
    leading = lower_rows.shape[:2]
    slot_total = leading[0] * leading[1]
    extent = lower_rows.shape[2]
    across = tile_image.shape[1]
    channels = tile_image.shape[2]
    low_blocks = lower_rows.reshape(slot_total // 8, 8, extent)
    lw_blocks = lower_weight.reshape(slot_total // 8, 8, extent)
    uw_blocks = upper_weight.reshape(slot_total // 8, 8, extent)
    col_blocks = col_weights.reshape(slot_total // 8, 8, extent, across)

    def sample_one_block(members):
        low_part, lw_part, uw_part, col_part = members
        lower_taken = jnp.take(tile_image, low_part, axis=0).astype(jnp.float32)
        upper_taken = jnp.take(tile_image, low_part + 1, axis=0).astype(jnp.float32)
        stripes = (
            lw_part.astype(jnp.float32)[..., None, None] * lower_taken
            + uw_part.astype(jnp.float32)[..., None, None] * upper_taken
        ).astype(jnp.bfloat16)
        return jnp.einsum(
            "sqx,spxc->spqc", col_part, stripes, preferred_element_type=jnp.float32
        ).astype(jnp.bfloat16)

    sampled = lax.map(sample_one_block, (low_blocks, lw_blocks, uw_blocks, col_blocks))
    return sampled.reshape(leading + (extent, extent, channels))


def spread_blocks(slot_grads, lower_rows, lower_weight, upper_weight, col_weights, height):
    leading = lower_rows.shape[:2]
    slot_total = leading[0] * leading[1]
    extent = lower_rows.shape[2]
    across = col_weights.shape[3]
    channels = slot_grads.shape[-1]
    low_blocks = lower_rows.reshape(slot_total // 8, 8, extent)
    lw_blocks = lower_weight.reshape(slot_total // 8, 8, extent)
    uw_blocks = upper_weight.reshape(slot_total // 8, 8, extent)
    col_blocks = col_weights.reshape(slot_total // 8, 8, extent, across)
    grad_blocks = slot_grads.reshape(slot_total // 8, 8, extent, extent, channels)

    def spread_one_block(running_sum, members):
        low_part, lw_part, uw_part, col_part, grad_part = members
        stripes = jnp.einsum(
            "sqx,spqc->spxc", col_part, grad_part, preferred_element_type=jnp.float32
        ).astype(jnp.bfloat16)
        stripes_wide = stripes.astype(jnp.float32)
        lower_terms = (lw_part.astype(jnp.float32)[..., None, None] * stripes_wide).reshape(
            -1, across, channels
        )
        upper_terms = (uw_part.astype(jnp.float32)[..., None, None] * stripes_wide).reshape(
            -1, across, channels
        )
        flat_rows = low_part.reshape(-1)
        running_sum = running_sum.at[flat_rows].add(lower_terms)
        running_sum = running_sum.at[flat_rows + 1].add(upper_terms)
        return (running_sum, None)

    initial = jnp.zeros((height, across, channels), jnp.float32)
    summed, unused = lax.scan(
        spread_one_block, initial, (low_blocks, lw_blocks, uw_blocks, col_blocks, grad_blocks)
    )
    return summed.astype(jnp.bfloat16)


def unfold(values):
    region_count = values.shape[0]
    extent = values.shape[1]
    channels = values.shape[3]
    padded = jnp.pad(values, ((0, 0), (1, 1), (1, 1), (0, 0)))
    pieces = [
        padded[:, row_off : row_off + extent, col_off : col_off + extent, :]
        for row_off in range(3)
        for col_off in range(3)
    ]
    return jnp.concatenate(pieces, axis=-1).reshape(region_count * extent * extent, 9 * channels)


def refold(columns, region_count, extent, channels):
    pieces = columns.reshape(region_count, extent, extent, 9, channels)
    padded = jnp.zeros((region_count, extent + 2, extent + 2, channels), jnp.float32)
    for row_off in range(3):
        for col_off in range(3):
            padded = padded.at[:, row_off : row_off + extent, col_off : col_off + extent, :].add(
                pieces[:, :, :, 3 * row_off + col_off, :]
            )
    return padded[:, 1:-1, 1:-1, :]


def silu_slope(values):
    sigma = jax.nn.sigmoid(values)
    return sigma * (1.0 + values * (1.0 - sigma))


def region_pass(inputs, upstream, first_kernel, second_kernel):
    region_count = inputs.shape[0]
    extent = inputs.shape[1]
    channels = inputs.shape[3]
    first_flat = first_kernel.reshape(9 * channels, channels)
    second_flat = second_kernel.reshape(9 * channels, channels)
    contract_rows = (((0,), (0,)), ((), ()))
    contract_last = (((1,), (1,)), ((), ()))
    input_cols = unfold(inputs)
    first_pre = jnp.dot(input_cols, first_flat, preferred_element_type=jnp.float32)
    hidden = jax.nn.silu(first_pre).astype(jnp.bfloat16)
    hidden_cols = unfold(hidden.reshape(region_count, extent, extent, channels))
    second_pre = jnp.dot(hidden_cols, second_flat, preferred_element_type=jnp.float32)
    second_delta = (
        upstream.reshape(-1, channels).astype(jnp.float32) * silu_slope(second_pre)
    ).astype(jnp.bfloat16)
    second_raw = lax.dot_general(
        hidden_cols, second_delta, contract_rows, preferred_element_type=jnp.float32
    )
    hidden_cols_back = lax.dot_general(
        second_delta, second_flat, contract_last, preferred_element_type=jnp.float32
    )
    hidden_back = refold(hidden_cols_back, region_count, extent, channels)
    first_delta = (hidden_back.reshape(-1, channels) * silu_slope(first_pre)).astype(jnp.bfloat16)
    first_raw = lax.dot_general(
        input_cols, first_delta, contract_rows, preferred_element_type=jnp.float32
    )
    input_cols_back = lax.dot_general(
        first_delta, first_flat, contract_last, preferred_element_type=jnp.float32
    )
    input_back = refold(input_cols_back, region_count, extent, channels).astype(jnp.bfloat16)
    return (input_back, first_raw, second_raw)


def compact_plan(active, region_total):
    live_flags = active.reshape(-1)
    running = jnp.cumsum(live_flags.astype(jnp.int32), dtype=jnp.int32)
    region_ids = jnp.arange(region_total, dtype=jnp.int32)
    chosen = jnp.sum(
        (running[None, :] <= region_ids[:, None]).astype(jnp.int32), axis=1, dtype=jnp.int32
    )
    placed = jnp.maximum(running - 1, 0)
    return (chosen, placed, live_flags)


def on_device(features, out_grad, pair_count, sample_grid, first_kernel, second_kernel):
    tile_count = lax.axis_size("tile")
    own_index = lax.axis_index("tile")
    tile_image = features[0]
    height = tile_image.shape[0]
    across = tile_image.shape[1]
    channels = tile_image.shape[2]
    counts = pair_count[0]
    slot_grid = sample_grid[0, 0]
    capacity = slot_grid.shape[1]
    extent = slot_grid.shape[3]
    upstream = out_grad[0]
    region_total = upstream.shape[0]
    slot_ids = jnp.arange(capacity, dtype=jnp.int32)
    send_counts = lax.dynamic_index_in_dim(counts, own_index, 0, keepdims=False)
    send_active = slot_ids[None, :] < send_counts[:, None]
    lower_rows = slot_grid[..., 0, :]
    upper_share = slot_grid[..., 1, :].astype(jnp.float32) / 16.0
    live_scale = send_active[..., None].astype(jnp.float32)
    lower_weight = ((1.0 - upper_share) * live_scale).astype(jnp.bfloat16)
    upper_weight = (upper_share * live_scale).astype(jnp.bfloat16)
    col_weights = column_weights(slot_grid, across)
    sent_blocks = sample_blocks(tile_image, lower_rows, lower_weight, upper_weight, col_weights)
    arrived = lax.all_to_all(sent_blocks, "tile", split_axis=0, concat_axis=0, tiled=True)
    recv_counts = lax.dynamic_index_in_dim(counts, own_index, 1, keepdims=False)
    recv_active = slot_ids[None, :] < recv_counts[:, None]
    chosen, placed, live_flags = compact_plan(recv_active, region_total)
    inputs = jnp.take(
        arrived.reshape(tile_count * capacity, extent, extent, channels), chosen, axis=0
    )
    input_back, first_raw, second_raw = region_pass(inputs, upstream, first_kernel, second_kernel)
    taken_back = jnp.take(input_back, placed, axis=0)
    slot_back = jnp.where(live_flags[:, None, None, None], taken_back, jnp.zeros_like(taken_back))
    slot_back = slot_back.reshape(tile_count, capacity, extent, extent, channels)
    returned = lax.all_to_all(slot_back, "tile", split_axis=0, concat_axis=0, tiled=True)
    image_grads = spread_blocks(
        returned, lower_rows, lower_weight, upper_weight, col_weights, height
    )
    first_total, second_total = lax.psum((first_raw, second_raw), ("tile", "group"))
    grad_scale = 1.0 / math.sqrt(
        lax.axis_size("group") * tile_count * region_total * extent * extent
    )
    first_grad = (first_total * grad_scale).reshape(3, 3, channels, channels)
    second_grad = (second_total * grad_scale).reshape(3, 3, channels, channels)
    return (image_grads[None], first_grad, second_grad)


def solution(mesh):
    return jax.shard_map(
        on_device,
        mesh=mesh,
        in_specs=(
            P("group", "tile", None, None),
            P("group", "tile", None, None, None),
            P("group", None, None),
            P("group", "tile", None, None, None, None),
            P(),
            P(),
        ),
        out_specs=(P("group", "tile", None, None), P(), P()),
        check_vma=False,
    )
```

profile of v0, /device:TPU:1, one launch (start us, length us, event | category | flops | bytes accessed | tf_op | source)
XLA Modules:
  0.0 975.2 jit_solution(4552191681005784622)
XLA Ops:
  10.7 76.9 %while.40 = (s32[]{:T(128)}, bf16[8,8,14,14,256]{4,3,2,1,0:T(8,128)(2,1)}, bf16[8,8,14]{2,1,0:T(8,128)(2,1)S(1)}, s32[8,8,14]{2,1,0:T(8,128)S(1)}, bf16[64,32,25...) while((s32[]{:T(128)}, ...), condition=%wide.region_3.5_spmd, body=%wide.region_2.4_spmd.sunk | while | flops 33435280 | bytes 16180697 | solution.py:44
  124.0 59.4 %all-to-all-done = bf16[32,2,14,14,256]{4,1,3,2,0:T(2,128)(2,1)} async-done(((bf16[32,2,14,14,256]{4,1,3,2,0:T(2,128)(2,1)}), bf16[32,2,14,14,256]{4,1,3,2,0:T(2,128)(2,1)}, u32[]{:S(2)}, u32[]{:S(2)}) %all-to-all-start) | async-done | bytes 6422560 | tf_op jit(solution)/shard_map/all_to_all | solution.py:181
  219.8 29.7 %reshape.1063 = bf16[4312,2304]{1,0:T(8,128)(2,1)} reshape(bf16[22,14,14,2304]{3,2,1,0:T(8,128)(2,1)} %slice_dynamic-update-slice_fusion) | data formatting | bytes 39739392 | tf_op jit(solution)/shard_map/reshape | solution.py:94
  263.1 15.1 %pad_slice_fusion = (bf16[22,14,14,256]{3,2,1,0:T(8,128)(2,1)}, bf16[22,14,14,256]{3,2,1,0:T(8,128)(2,1)}, bf16[22,14,14,256]{3,2,1,0:T(8,128)(2,1)}, bf16[22,14...) fusion(bf16[22,14,14,256]{3,2,1,0:T(8,128)(2,1)} %reshape.1065), kind=kLoop, calls=%fused_computation.118 | loop fusion | bytes 19869696 | tf_op jit(solution)/shard_map/slice | solution.py:90
  334.0 11.9 %multiply_convert_fusion.1 = (bf16[4312,256]{1,0:T(8,128)(2,1)S(1)}, f32[4312,256]{1,0:T(8,128)}) fusion(f32[4312,256]{1,0:T(8,128)S(1)} %bitcast.256, bf16[4312,2304]{1,0:T(8,128)(2,1)} %constant_dynamic-update-slice_fusion.1, bf16[2304,256]{1,0:T(8,128)(2,1)S(1)} %bitcast.244), kind=kOutput, calls=%fused_computation.100 | convolution fusion | flops 5096577024 | bytes 32088064 | tf_op jit(solution)/shard_map/dot_general | solution.py:125
  348.0 18.5 %fusion.54 = f32[22,14,14,9,256]{4,0,3,2,1:T(8,128)} fusion(bf16[9,256,256,1,1]{2,1,0,4,3:T(8,128)(2,1)S(1)} %bitcast.243, bf16[22,14,14,256,1]{3,2,1,0,4:T(8,128)(2,1)} %bitcast.253), kind=kOutput, calls=%fused_computation.114 | convolution fusion | flops 5086642176 | bytes 43126784 | tf_op jit(solution)/shard_map/dot_general | solution.py:132
  417.6 18.5 %fusion.52 = f32[22,14,14,9,256]{4,0,2,1,3:T(8,128)} fusion(bf16[9,256,256,1,1]{2,1,4,3,0:T(8,128)(2,1)S(1)} %bitcast.260, bf16[22,14,14,256]{3,2,1,0:T(8,128)(2,1)} %dot_general.40), kind=kOutput, calls=%fused_computation.112 | convolution fusion | flops 5086642176 | bytes 43126784 | tf_op jit(solution)/shard_map/dot_general | solution.py:140
  478.0 12.2 %broadcast_select_fusion.1 = bf16[32,2,14,14,256]{4,1,3,2,0:T(2,128)(2,1)} fusion(pred[32,2]{1,0:T(8,128)(4,1)S(1)} %copy-done.14, pred[32,2]{1,0:T(8,128)(4,1)S(1)} %copy-done.13, bf16[32,2,14,14,256]{4,3,2,1,0:T(8,128)(2,1)} %bitcast.250), kind=kLoop, calls=%fused_computation.47 | loop fusion | flops 6422528 | bytes 12845184 | tf_op jit(solution)/shard_map/jit(_where)/select_n | solution.py:190
  511.3 13.3 %fusion.57 = f32[2304,256]{1,0:T(8,128)} fusion(bf16[4312,2304]{1,0:T(8,128)(2,1)} %constant_dynamic-update-slice_fusion.1, f32[4312,256]{1,0:T(8,128)} %reshape.1096, f32[4312,256]{1,0:T(8,128)} %get-tuple-element.451), kind=kOutput, calls=%fused_computation.117 | convolution fusion | flops 5096577024 | bytes 31059968 | tf_op jit(solution)/shard_map/dot_general | solution.py:129
  524.6 187.9 %all-reduce.7.cloned.1.call-done = (f32[2304,256]{1,0:T(8,128)}, f32[2304,256]{1,0:T(8,128)}) async-done(((f32[2304,256]{1,0:T(8,128)}, f32[2304,256]{1,0:T(8,128)}), (f32[2304,256]{1,0:T(8,128)}, f32[2304,256]{1,0:T(8,128)})) %all-reduce.7.cloned.1.call-update) | async-done | bytes 4718608 | tf_op jit(solution)/shard_map/psum | solution.py:196
  724.9 241.6 %while.41 = (s32[]{:T(128)}, f32[64,32,256]{2,1,0:T(8,128)S(1)}, s32[8,8,14]{2,1,0:T(8,128)}, bf16[8,8,14]{2,1,0:T(8,128)(2,1)}, bf16[8,8,14,14,256]{4,3,2,1,0:T...) while((s32[]{:T(128)}, f32[64,32,256]{2,1,0:T(8,128)S(1)}, ...), condition=%wide.region_8.10_spmd, body=%wide.region_5.9_spmd.sunk | while | flops 31196144 | bytes 30317788 | solution.py:78
  731.4 11.9 %scatter_fusion = f32[64,32,256]{2,1,0:T(8,128)S(1)} fusion(f32[64,32,256]{2,1,0:T(8,128)S(1)} %get-tuple-element.597, s32[112]{0:T(128)S(1)} %get-tuple-element.558, f32[112,32,256]{2,1,0:T(8,128)} %bitcast.246), kind=kCustom, calls=%fused_computation.4.clone.1 | custom fusion | flops 917504 | bytes 11010496 | tf_op jit(solution)/shard_map/while/body/eval_jaxpr/scatter-add | solution.py:73
  743.3 11.9 %scatter_fusion.1 = f32[64,32,256]{2,1,0:T(8,128)S(1)} fusion(f32[64,32,256]{2,1,0:T(8,128)S(1)} %scatter_fusion, s32[112]{0:T(128)S(1)} %get-tuple-element.562, f32[112,32,256]{2,1,0:T(8,128)} %bitcast.245), kind=kCustom, calls=%fused_computation.5.clone.1 | custom fusion | flops 917504 | bytes 11010496 | tf_op jit(solution)/shard_map/while/body/eval_jaxpr/scatter-add | solution.py:74
  761.6 11.8 %scatter_fusion = f32[64,32,256]{2,1,0:T(8,128)S(1)} fusion(f32[64,32,256]{2,1,0:T(8,128)S(1)} %get-tuple-element.597, s32[112]{0:T(128)S(1)} %get-tuple-element.558, f32[112,32,256]{2,1,0:T(8,128)} %bitcast.246), kind=kCustom, calls=%fused_computation.4.clone.1 | custom fusion | flops 917504 | bytes 11010496 | tf_op jit(solution)/shard_map/while/body/eval_jaxpr/scatter-add | solution.py:73
  791.8 11.9 %scatter_fusion = f32[64,32,256]{2,1,0:T(8,128)S(1)} fusion(f32[64,32,256]{2,1,0:T(8,128)S(1)} %get-tuple-element.597, s32[112]{0:T(128)S(1)} %get-tuple-element.558, f32[112,32,256]{2,1,0:T(8,128)} %bitcast.246), kind=kCustom, calls=%fused_computation.4.clone.1 | custom fusion | flops 917504 | bytes 11010496 | tf_op jit(solution)/shard_map/while/body/eval_jaxpr/scatter-add | solution.py:73
  803.7 11.9 %scatter_fusion.1 = f32[64,32,256]{2,1,0:T(8,128)S(1)} fusion(f32[64,32,256]{2,1,0:T(8,128)S(1)} %scatter_fusion, s32[112]{0:T(128)S(1)} %get-tuple-element.562, f32[112,32,256]{2,1,0:T(8,128)} %bitcast.245), kind=kCustom, calls=%fused_computation.5.clone.1 | custom fusion | flops 917504 | bytes 11010496 | tf_op jit(solution)/shard_map/while/body/eval_jaxpr/scatter-add | solution.py:74
  822.0 11.9 %scatter_fusion = f32[64,32,256]{2,1,0:T(8,128)S(1)} fusion(f32[64,32,256]{2,1,0:T(8,128)S(1)} %get-tuple-element.597, s32[112]{0:T(128)S(1)} %get-tuple-element.558, f32[112,32,256]{2,1,0:T(8,128)} %bitcast.246), kind=kCustom, calls=%fused_computation.4.clone.1 | custom fusion | flops 917504 | bytes 11010496 | tf_op jit(solution)/shard_map/while/body/eval_jaxpr/scatter-add | solution.py:73
  833.9 11.9 %scatter_fusion.1 = f32[64,32,256]{2,1,0:T(8,128)S(1)} fusion(f32[64,32,256]{2,1,0:T(8,128)S(1)} %scatter_fusion, s32[112]{0:T(128)S(1)} %get-tuple-element.562, f32[112,32,256]{2,1,0:T(8,128)} %bitcast.245), kind=kCustom, calls=%fused_computation.5.clone.1 | custom fusion | flops 917504 | bytes 11010496 | tf_op jit(solution)/shard_map/while/body/eval_jaxpr/scatter-add | solution.py:74
  882.4 11.8 %scatter_fusion = f32[64,32,256]{2,1,0:T(8,128)S(1)} fusion(f32[64,32,256]{2,1,0:T(8,128)S(1)} %get-tuple-element.597, s32[112]{0:T(128)S(1)} %get-tuple-element.558, f32[112,32,256]{2,1,0:T(8,128)} %bitcast.246), kind=kCustom, calls=%fused_computation.4.clone.1 | custom fusion | flops 917504 | bytes 11010496 | tf_op jit(solution)/shard_map/while/body/eval_jaxpr/scatter-add | solution.py:73
  894.3 11.8 %scatter_fusion.1 = f32[64,32,256]{2,1,0:T(8,128)S(1)} fusion(f32[64,32,256]{2,1,0:T(8,128)S(1)} %scatter_fusion, s32[112]{0:T(128)S(1)} %get-tuple-element.562, f32[112,32,256]{2,1,0:T(8,128)} %bitcast.245), kind=kCustom, calls=%fused_computation.5.clone.1 | custom fusion | flops 917504 | bytes 11010496 | tf_op jit(solution)/shard_map/while/body/eval_jaxpr/scatter-add | solution.py:74
  912.6 11.9 %scatter_fusion = f32[64,32,256]{2,1,0:T(8,128)S(1)} fusion(f32[64,32,256]{2,1,0:T(8,128)S(1)} %get-tuple-element.597, s32[112]{0:T(128)S(1)} %get-tuple-element.558, f32[112,32,256]{2,1,0:T(8,128)} %bitcast.246), kind=kCustom, calls=%fused_computation.4.clone.1 | custom fusion | flops 917504 | bytes 11010496 | tf_op jit(solution)/shard_map/while/body/eval_jaxpr/scatter-add | solution.py:73
  924.4 11.9 %scatter_fusion.1 = f32[64,32,256]{2,1,0:T(8,128)S(1)} fusion(f32[64,32,256]{2,1,0:T(8,128)S(1)} %scatter_fusion, s32[112]{0:T(128)S(1)} %get-tuple-element.562, f32[112,32,256]{2,1,0:T(8,128)} %bitcast.245), kind=kCustom, calls=%fused_computation.5.clone.1 | custom fusion | flops 917504 | bytes 11010496 | tf_op jit(solution)/shard_map/while/body/eval_jaxpr/scatter-add | solution.py:74
  942.8 11.9 %scatter_fusion = f32[64,32,256]{2,1,0:T(8,128)S(1)} fusion(f32[64,32,256]{2,1,0:T(8,128)S(1)} %get-tuple-element.597, s32[112]{0:T(128)S(1)} %get-tuple-element.558, f32[112,32,256]{2,1,0:T(8,128)} %bitcast.246), kind=kCustom, calls=%fused_computation.4.clone.1 | custom fusion | flops 917504 | bytes 11010496 | tf_op jit(solution)/shard_map/while/body/eval_jaxpr/scatter-add | solution.py:73
  954.6 11.9 %scatter_fusion.1 = f32[64,32,256]{2,1,0:T(8,128)S(1)} fusion(f32[64,32,256]{2,1,0:T(8,128)S(1)} %scatter_fusion, s32[112]{0:T(128)S(1)} %get-tuple-element.562, f32[112,32,256]{2,1,0:T(8,128)} %bitcast.245), kind=kCustom, calls=%fused_computation.5.clone.1 | custom fusion | flops 917504 | bytes 11010496 | tf_op jit(solution)/shard_map/while/body/eval_jaxpr/scatter-add | solution.py:74
  (283 shorter events, 439.5 us)
Async XLA Ops:
  7.2 326.6 %copy-start = (bf16[3,3,256,256]{3,2,1,0:T(8,128)(2,1)S(1)}, bf16[3,3,256,256]{3,2,1,0:T(8,128)(2,1)}, u32[]{:S(2)}) copy-start(bf16[3,3,256,256]{3,2,1,0:T(8,128)(2,1)} %param.53) | copy-start | bytes 3538948
  10.8 3.5 copy-start.2
  20.4 3.5 copy-start.2
  30.0 3.5 copy-start.2
  39.6 3.5 copy-start.2
  49.2 3.5 copy-start.2
  58.8 3.5 copy-start.2
  68.5 3.5 copy-start.2
  78.1 3.5 copy-start.2
  87.7 11.0 %copy-start.9 = (bf16[8,8,14,32]{3,2,1,0:T(8,128)(2,1)}, bf16[8,8,14,32]{3,2,1,0:T(8,128)(2,1)S(1)}, u32[]{:S(2)}) copy-start(bf16[8,8,14,32]{3,2,1,0:T(8,128)(2,1)S(1)} %get-tuple-element.626) | copy-start | bytes 172036
  87.7 11.0 %copy-start.10 = (s32[8,8,14]{2,1,0:T(8,128)}, s32[8,8,14]{2,1,0:T(8,128)S(1)}, u32[]{:S(2)}) copy-start(s32[8,8,14]{2,1,0:T(8,128)S(1)} %get-tuple-element.627) | copy-start | bytes 10756
  87.7 11.0 %copy-start.11 = (bf16[8,8,14]{2,1,0:T(8,128)(2,1)}, bf16[8,8,14]{2,1,0:T(8,128)(2,1)S(1)}, u32[]{:S(2)}) copy-start(bf16[8,8,14]{2,1,0:T(8,128)(2,1)S(1)} %get-tuple-element.628) | copy-start | bytes 5380
  87.7 11.0 %copy-start.12 = (bf16[8,8,14]{2,1,0:T(8,128)(2,1)}, bf16[8,8,14]{2,1,0:T(8,128)(2,1)S(1)}, u32[]{:S(2)}) copy-start(bf16[8,8,14]{2,1,0:T(8,128)(2,1)S(1)} %get-tuple-element.629) | copy-start | bytes 5380
  98.7 10.2 %copy-start.15 = (s32[1,32,32]{2,1,0:T(8,128)S(1)}, s32[1,32,32]{2,1,0:T(8,128)}, u32[]{:S(2)}) copy-start(s32[1,32,32]{2,1,0:T(8,128)} %param.50) | copy-start | bytes 12292
  98.8 84.7 %all-to-all-start = ((bf16[32,2,14,14,256]{4,1,3,2,0:T(2,128)(2,1)}), bf16[32,2,14,14,256]{4,1,3,2,0:T(2,128)(2,1)}, u32[]{:S(2)}, u32[]{:S(2)}) async-start(bf16[32,2,14,14,256]{4,1,3,2,0:T(2,128)(2,1)} %copy.264), calls=%async_computation | async-start | bytes 12845056 | tf_op jit(solution)/shard_map/all_to_all | solution.py:181
  114.6 8.7 copy-start.16
  202.6 5.3 copy-start.3
  300.0 3.4 copy-start.7
  300.0 5.0 copy-start.6
  328.9 4.8 slice-start
  472.2 5.8 copy-start.13
  472.2 5.8 copy-start.14
  490.2 227.3 %all-to-all-start.1 = ((bf16[32,2,14,14,256]{4,1,3,2,0:T(2,128)(2,1)}), bf16[32,2,14,14,256]{4,1,3,2,0:T(2,128)(2,1)}, u32[]{:S(2)}, u32[]{:S(2)}) async-start(bf16[32,2,14,14,256]{4,1,3,2,0:T(2,128)(2,1)} %broadcast_select_fusion.1), calls=%async_computation.1 | async-start | bytes 12845056 | tf_op jit(solution)/shard_map/all_to_all | solution.py:192
  500.0 212.5 %all-reduce.7.cloned.1.call-start = ((), (), s32[]{:S(2)}) async-start(), calls=%async_computation.2 | async-start | bytes 9437184 | tf_op jit(solution)/shard_map/psum | solution.py:196
  (5 other events, 13.8 us)
Sparse Core Ops, SparseCore 0:
  524.7 187.7 all-reduce.6
where the time goes:
time: 988 us; the launch traced here: 975 us
  other arithmetic  288 us (29%)
  local copies, waits for them, and re-layouts  247 us (25%)
  waiting for transfers between devices  247 us (25%)
  matrix products  158 us (16%)
  starting transfers between devices  19.9 us (2%)
  between operations  14.6 us (1%)
    psum x1, waiting for transfers between devices, on_device(): lax.psum((first_raw, second_raw), ('tile', 'group'))  188 us
    scatter-add x8, other arithmetic, spread_one_block(): running_sum = running_sum.at[flat_rows].add(lower_terms)  94.8 us
    scatter-add x8, other arithmetic, spread_one_block(): running_sum = running_sum.at[flat_rows + 1].add(upper_terms)  94.8 us
    scatter-add x16, other arithmetic, refold(): padded.at[:, row_off:row_off + extent, col_off:col_off + extent, :]  61.3 us
    all_to_all x1, waiting for transfers between devices, on_device(): lax.all_to_all(sent_blocks, 'tile', split_axis=0, concat_axis=0, tiled=True)  59.4 us
    dot_general x8, matrix products, spread_one_block(): jnp.einsum('sqx,spqc->spxc', col_part, grad_part, preferred_element_type=...  40.2 us
    concatenate x10, local copies, waits for them, and re-layouts, unfold(): jnp.concatenate(pieces, axis=-1)  39.8 us
    unnamed x52, local copies, waits for them, and re-layouts  36.6 us
  transfers between devices with their start and end apart: 3, of which 2 were waited for; matrix products, arithmetic and copies ran while one was open for 5% of the time, Pallas kernels for 0%

commit v1 on v0

v1 whole, which is shorter than its diff:
```python
import functools
import math

import jax
import jax.numpy as jnp
from jax import lax
from jax.experimental import pallas as pl
from jax.experimental.pallas import tpu as pltpu
from jax.sharding import PartitionSpec as P

BF = jnp.bfloat16
F32 = jnp.float32
MESH = pl.DeviceIdType.MESH
RES = 14
PITCH = 16
FLAT = RES * PITCH
PACK = 200
CH = 256
WIDE = 3 * CH
TH = 64
TW = 32
VMEM = 60 * 1024 * 1024


def iota(shape, dim):
    return lax.broadcasted_iota(jnp.int32, shape, dim)


def dot(a, b):
    return jnp.dot(a, b, preferred_element_type=F32)


def packed_place(col):
    return jnp.where((col & 15) < RES, (col >> 4) * RES + (col & 15), -1)


def pack_kernel(place_ref, grad_ref, out_ref, padded, packed, sems):
    regions = grad_ref.shape[0]
    padded[...] = jnp.zeros_like(padded)
    perm = (iota((PACK, FLAT), 0) == packed_place(iota((PACK, FLAT), 1))).astype(F32).astype(BF)
    copies = []
    for k in range(regions):
        padded[k % 2, :, 0:RES, :] = grad_ref[k]
        flat = padded[k % 2].reshape(FLAT, CH)
        packed[k] = dot(perm, flat).astype(BF)
        copy = pltpu.make_async_copy(packed.at[k], out_ref.at[place_ref[k]], sems.at[k])
        copy.start()
        copies.append(copy)
    for copy in copies:
        copy.wait()


def pack_upstream(place, upstream, slots):
    regions = upstream.shape[0]
    return pl.pallas_call(
        pack_kernel,
        grid_spec=pltpu.PrefetchScalarGridSpec(
            num_scalar_prefetch=1,
            grid=(1,),
            in_specs=[pl.BlockSpec(upstream.shape, lambda i, p: (0, 0, 0, 0))],
            out_specs=pl.BlockSpec(memory_space=pl.ANY),
            scratch_shapes=[
                pltpu.VMEM((2, RES, PITCH, CH), BF),
                pltpu.VMEM((regions, PACK, CH), BF),
                pltpu.SemaphoreType.DMA((regions,)),
            ],
        ),
        out_shape=jax.ShapeDtypeStruct((slots, PACK, CH), BF),
        compiler_params=pltpu.CompilerParams(vmem_limit_bytes=VMEM),
    )(place, upstream)


def put_shifted(ref, r, value):
    ref[r, PITCH : PITCH + FLAT, 0:CH] = pltpu.roll(value, 1, 0).astype(BF)
    ref[r, PITCH : PITCH + FLAT, CH : 2 * CH] = value.astype(BF)
    ref[r, PITCH : PITCH + FLAT, 2 * CH : WIDE] = pltpu.roll(value, FLAT - 1, 0).astype(BF)


def clear_edges(ref):
    edge = jnp.zeros((ref.shape[0], PITCH, WIDE), BF)
    ref[:, 0:PITCH, :] = edge
    ref[:, PITCH + FLAT : 2 * PITCH + FLAT, :] = edge


def conv(ref, r, kernel_ref):
    total = dot(ref[r, 0:FLAT, :], kernel_ref[0])
    total += dot(ref[r, PITCH : PITCH + FLAT, :], kernel_ref[1])
    total += dot(ref[r, 2 * PITCH : 2 * PITCH + FLAT, :], kernel_ref[2])
    return total


def sampled_block(geo_ref, slot, tile_ref):
    row0, row_step = geo_ref[slot * 4], geo_ref[slot * 4 + 1]
    col0, col_step = geo_ref[slot * 4 + 2], geo_ref[slot * 4 + 3]
    lane, sub = iota((PITCH, CH), 1), iota((PITCH, CH), 0)
    reach = 16 - jnp.abs(16 * (lane & 31) - (col0 + col_step * sub))
    col_weight = jnp.where(sub < RES, jnp.maximum(reach, 0), 0).astype(F32)
    lower = (lane & 32) == 0
    owner = lane >> 6
    pieces = []
    for first in range(0, RES, 4):
        members = range(first, min(first + 4, RES))
        weights, rows = [], []
        for p in members:
            place = row0 + row_step * p
            low = place >> 4
            share = (place & 15).astype(F32) * (1.0 / 256.0)
            row_weight = jnp.where(lower, 1.0 / 16.0 - share, share)
            weights.append(jnp.where(owner == p - first, row_weight * col_weight, 0.0).astype(BF))
            rows.append(tile_ref[pl.ds(low, 2)].reshape(2 * TW, CH))
        depth = 64 * len(rows)
        left = jnp.concatenate(weights, axis=0)[:, 0:depth]
        pieces.append(dot(left, jnp.concatenate(rows, axis=0)))
    return jnp.concatenate(pieces, axis=0)


def sigmoid(v):
    return 0.5 * jnp.tanh(0.5 * v) + 0.5


def forward_kernel(steps_ref, *refs):
    wide_in, wide_hid = refs[-2:]

    @pl.when(pl.program_id(0) == 0)
    def _():
        clear_edges(wide_in)
        clear_edges(wide_hid)

    pl.when(pl.program_id(0) < steps_ref[0])(functools.partial(forward_step, *refs))


def forward_step(list_ref, geo_ref, tile_ref, first_ref, second_ref, out_ref, wide_in, wide_hid):
    step = pl.program_id(0)
    per = out_ref.shape[0]
    inside = (iota((FLAT, CH), 0) & 15) < RES
    for r in range(per):
        slot = list_ref[step * per + r]
        block = sampled_block(geo_ref, slot, tile_ref)
        put_shifted(wide_in, r, block)
        out_ref[r, 0] = block.astype(BF)
    for r in range(per):
        pre = conv(wide_in, r, first_ref)
        gate = sigmoid(pre)
        hidden = jnp.where(inside, pre * gate, 0.0)
        put_shifted(wide_hid, r, hidden)
        out_ref[r, 1] = hidden.astype(BF)
        out_ref[r, 2] = jnp.where(inside, gate * (1.0 + pre * (1.0 - gate)), 0.0).astype(BF)
    for r in range(per):
        pre = conv(wide_hid, r, second_ref)
        gate = sigmoid(pre)
        out_ref[r, 3] = (gate * (1.0 + pre * (1.0 - gate))).astype(BF)


PER = 2


def held(step, steps_ref):
    return jnp.minimum(step, steps_ref[0] - 1)


def forward(steps, slots, geo, tile, first, second):
    count = slots.shape[0]
    whole = lambda *shape: pl.BlockSpec(shape, lambda i, *_: (0,) * len(shape))
    return pl.pallas_call(
        forward_kernel,
        grid_spec=pltpu.PrefetchScalarGridSpec(
            num_scalar_prefetch=3,
            grid=(count // PER,),
            in_specs=[whole(TH, TW, CH), whole(3, WIDE, CH), whole(3, WIDE, CH)],
            out_specs=pl.BlockSpec(
                (PER, 4, FLAT, CH), lambda i, n, *_: (held(i, n), 0, 0, 0)
            ),
            scratch_shapes=[
                pltpu.VMEM((PER, FLAT + 2 * PITCH, WIDE), BF),
                pltpu.VMEM((PER, FLAT + 2 * PITCH, WIDE), BF),
            ],
        ),
        out_shape=jax.ShapeDtypeStruct((count, 4, FLAT, CH), BF),
        compiler_params=pltpu.CompilerParams(vmem_limit_bytes=VMEM),
    )(steps, slots, geo, tile, first, second)


def spread(geo_ref, slot, back, grad_ref):
    row0, row_step = geo_ref[slot * 4], geo_ref[slot * 4 + 1]
    col0, col_step = geo_ref[slot * 4 + 2], geo_ref[slot * 4 + 3]
    up, along = iota((CH, 128), 0), iota((CH, 128), 1)
    reach = 16 - jnp.abs(16 * (up & 31) - (col0 + col_step * (along & 15)))
    live = ((along & 15) < RES) & ((up >> 5) == (along >> 4))
    weight = jnp.where(live, jnp.maximum(reach, 0), 0).astype(F32) * (1.0 / 16.0)
    weight = weight.astype(BF)
    for first in (0, 8):
        members = min(8, RES - first)
        stripes = dot(
            weight[0 : members * TW, 0 : members * PITCH],
            back[first * PITCH : (first + members) * PITCH],
        )
        for k in range(members):
            place = row0 + row_step * (first + k)
            low = place >> 4
            share = (place & 15).astype(F32) * (1.0 / 16.0)
            stripe = stripes[k * TW : (k + 1) * TW]
            grad_ref[low] = grad_ref[low] + (1.0 - share) * stripe
            grad_ref[low + 1] = grad_ref[low + 1] + share * stripe


def backward_kernel(
    steps_ref, list_ref, live_ref, geo_ref, kept_ref, up_a, up_b, first_ref, second_ref,
    tile_out, first_out, second_out,
    wide_two, wide_one, first_acc, second_acc, tile_acc, *, scale
):
    step = pl.program_id(0)

    @pl.when(step == 0)
    def _():
        clear_edges(wide_two)
        clear_edges(wide_one)
        first_acc[...] = jnp.zeros_like(first_acc)
        second_acc[...] = jnp.zeros_like(second_acc)
        tile_acc[...] = jnp.zeros_like(tile_acc)

    @pl.when(step < steps_ref[0])
    def _():
        backward_step(
            list_ref, live_ref, geo_ref, kept_ref, up_a, up_b, first_ref, second_ref,
            wide_two, wide_one, first_acc, second_acc, tile_acc,
        )

    @pl.when(step == pl.num_programs(0) - 1)
    def _():
        tile_out[...] = tile_acc[...].astype(BF)
        for a in range(3):
            for b in range(3):
                cols = slice((2 - b) * CH, (3 - b) * CH)
                first_out[a, b] = (first_acc[2 - a, :, cols] * scale).astype(first_out.dtype)
                second_out[a, b] = (second_acc[2 - a, :, cols] * scale).astype(second_out.dtype)


def backward_step(
    list_ref, live_ref, geo_ref, kept_ref, up_a, up_b, first_ref, second_ref,
    wide_two, wide_one, first_acc, second_acc, tile_acc
):
    step = pl.program_id(0)
    per = kept_ref.shape[0]
    unpack = (iota((FLAT, PACK), 1) == packed_place(iota((FLAT, PACK), 0))).astype(F32).astype(BF)
    across_rows = (((0,), (0,)), ((), ()))
    for r, up in enumerate((up_a, up_b)):
        live = live_ref[step * per + r] > 0
        packed = jnp.where(live, up[0], jnp.zeros_like(up[0]))
        put_shifted(wide_two, r, dot(unpack, packed) * kept_ref[r, 3].astype(F32))
    for a in range(3):
        for r in range(per):
            second_acc[a] += lax.dot_general(
                kept_ref[r, 1], wide_two[r, PITCH * a : PITCH * a + FLAT, :],
                across_rows, preferred_element_type=F32,
            )
    for r in range(per):
        put_shifted(wide_one, r, conv(wide_two, r, second_ref) * kept_ref[r, 2].astype(F32))
    for a in range(3):
        for r in range(per):
            first_acc[a] += lax.dot_general(
                kept_ref[r, 0], wide_one[r, PITCH * a : PITCH * a + FLAT, :],
                across_rows, preferred_element_type=F32,
            )
    for r in range(per):
        back = conv(wide_one, r, first_ref).astype(BF)
        spread(geo_ref, list_ref[step * per + r], back, tile_acc)


def backward(steps, slots, live, geo, kept, arrived, first_back, second_back, scale):
    whole = lambda *shape: pl.BlockSpec(shape, lambda i, *_: (0,) * len(shape))
    kernel_shape = jax.ShapeDtypeStruct((3, 3, CH, CH), BF)
    return pl.pallas_call(
        functools.partial(backward_kernel, scale=scale),
        grid_spec=pltpu.PrefetchScalarGridSpec(
            num_scalar_prefetch=4,
            grid=(slots.shape[0] // PER,),
            in_specs=[
                pl.BlockSpec((PER, 4, FLAT, CH), lambda i, n, *_: (held(i, n), 0, 0, 0)),
                pl.BlockSpec((1, PACK, CH), lambda i, n, s, *_: (s[PER * held(i, n)], 0, 0)),
                pl.BlockSpec((1, PACK, CH), lambda i, n, s, *_: (s[PER * held(i, n) + 1], 0, 0)),
                whole(3, WIDE, CH),
                whole(3, WIDE, CH),
            ],
            out_specs=[whole(TH, TW, CH), whole(3, 3, CH, CH), whole(3, 3, CH, CH)],
            scratch_shapes=[
                pltpu.VMEM((PER, FLAT + 2 * PITCH, WIDE), BF),
                pltpu.VMEM((PER, FLAT + 2 * PITCH, WIDE), BF),
                pltpu.VMEM((3, CH, WIDE), F32),
                pltpu.VMEM((3, CH, WIDE), F32),
                pltpu.VMEM((TH, TW, CH), F32),
            ],
        ),
        out_shape=[jax.ShapeDtypeStruct((TH, TW, CH), BF), kernel_shape, kernel_shape],
        compiler_params=pltpu.CompilerParams(vmem_limit_bytes=VMEM),
    )(steps, slots, live, geo, kept, arrived, arrived, first_back, second_back)


def reduce_kernel(planes, lines, mine_ref, out_ref, pair_in, half, shards, line_in, total, sems_s, sems_r):
    tile, line = lax.axis_index("tile"), lax.axis_index("group")
    core, chip = tile & 1, tile >> 1
    rows = mine_ref.shape[1]
    share = rows // planes
    other = (tile + 1) - 2 * core

    def plane_peer(k):
        return 2 * lax.rem(chip + k, planes) + core

    def line_peer(k):
        return lax.rem(line + k, lines)

    barrier = pltpu.get_barrier_semaphore()
    pl.semaphore_signal(barrier, inc=1, device_id={"tile": other}, device_id_type=MESH)

    def greet_plane(k, carry):
        pl.semaphore_signal(barrier, inc=1, device_id={"tile": plane_peer(k)}, device_id_type=MESH)
        return carry

    lax.fori_loop(1, planes, greet_plane, 0)
    for k in range(1, lines):
        pl.semaphore_signal(barrier, inc=1, device_id={"group": line_peer(k)}, device_id_type=MESH)
    pl.semaphore_wait(barrier, 1 + (planes - 1) + (lines - 1))

    swap = pltpu.make_async_remote_copy(
        mine_ref.at[1 - core], pair_in, sems_s.at[0], sems_r.at[0],
        device_id={"tile": other}, device_id_type=MESH,
    )
    swap.start()
    swap.wait()

    def add_pair(k, carry):
        at = pl.ds(pl.multiple_of(k * share, 16), share)
        half[at] = (mine_ref[core, at].astype(F32) + pair_in[at].astype(F32)).astype(BF)
        return carry

    lax.fori_loop(0, planes, add_pair, 0)

    def scatter(k):
        to = lax.rem(chip + k, planes)
        return pltpu.make_async_remote_copy(
            half.at[pl.ds(pl.multiple_of(to * share, 16), share)], shards.at[k - 1],
            sems_s.at[k], sems_r.at[k], device_id={"tile": 2 * to + core}, device_id_type=MESH,
        )

    def start_scatter(k, carry):
        scatter(k).start()
        return carry

    def wait_scatter(k, carry):
        scatter(k).wait()
        return carry

    lax.fori_loop(1, planes, start_scatter, 0)
    lax.fori_loop(1, planes, wait_scatter, 0)
    here = pl.ds(pl.multiple_of(chip * share, 16), share)
    partial = half[here].astype(F32)
    for k in range(planes - 1):
        partial += shards[k].astype(F32)
    total[...] = partial.astype(BF)

    moves = []
    for k in range(1, lines):
        move = pltpu.make_async_remote_copy(
            total, line_in.at[k - 1], sems_s.at[planes + k], sems_r.at[planes + k],
            device_id={"group": line_peer(k)}, device_id_type=MESH,
        )
        move.start()
        moves.append(move)
    for move in moves:
        move.wait()
    terms = [total[...].astype(F32)] + [line_in[k].astype(F32) for k in range(lines - 1)]
    final = None
    for position in range(lines):
        term = terms[0]
        for k in range(1, lines):
            term = jnp.where(lax.rem(line + lines - k, lines) == position, terms[k], term)
        final = term if final is None else final + term
    out_ref[core, here] = final.astype(BF)

    def gather(k, origin):
        at = pl.ds(pl.multiple_of(origin * share, 16), share)
        return pltpu.make_async_remote_copy(
            out_ref.at[core, at], out_ref.at[core, at],
            sems_s.at[planes + lines + k], sems_r.at[planes + lines + k],
            device_id={"tile": plane_peer(k)}, device_id_type=MESH,
        )

    def start_gather(k, carry):
        gather(k, chip).start()
        return carry

    def wait_gather(k, carry):
        gather(k, chip).wait_send()
        gather(k, lax.rem(chip - k + planes, planes)).wait_recv()
        return carry

    lax.fori_loop(1, planes, start_gather, 0)
    lax.fori_loop(1, planes, wait_gather, 0)

    last = pltpu.make_async_remote_copy(
        out_ref.at[core], out_ref.at[core], sems_s.at[planes], sems_r.at[planes],
        device_id={"tile": other}, device_id_type=MESH,
    )
    last.start()
    last.wait_send()
    pltpu.make_async_remote_copy(
        out_ref.at[1 - core], out_ref.at[1 - core], sems_s.at[planes], sems_r.at[planes],
        device_id={"tile": other}, device_id_type=MESH,
    ).wait_recv()


def reduce_everywhere(mine, tiles, lines):
    planes = tiles // 2
    rows = mine.shape[1]
    share = rows // planes
    spec = pl.BlockSpec(memory_space=pltpu.VMEM)
    return pl.pallas_call(
        functools.partial(reduce_kernel, planes, lines),
        in_specs=[spec],
        out_specs=spec,
        out_shape=jax.ShapeDtypeStruct(mine.shape, BF),
        scratch_shapes=[
            pltpu.VMEM((rows, CH), BF),
            pltpu.VMEM((rows, CH), BF),
            pltpu.VMEM((planes - 1, share, CH), BF),
            pltpu.VMEM((lines - 1, share, CH), BF),
            pltpu.VMEM((share, CH), BF),
            pltpu.SemaphoreType.DMA((2 * planes + lines,)),
            pltpu.SemaphoreType.DMA((2 * planes + lines,)),
        ],
        compiler_params=pltpu.CompilerParams(
            collective_id=0, has_side_effects=True, vmem_limit_bytes=VMEM
        ),
    )(mine)


def turned(kernel):
    return jnp.transpose(kernel[::-1, ::-1], (0, 1, 3, 2)).reshape(3, WIDE, CH)


def send_plan(column, regions):
    owners = column.shape[0]
    ids = jnp.arange(owners, dtype=jnp.int32)
    before = jnp.sum(jnp.where(ids[None, :] < ids[:, None], column[None, :], 0), axis=1)
    k = jnp.arange(regions, dtype=jnp.int32)[:, None]
    mine = (before[None, :] <= k) & (k < (before + column)[None, :])
    spot = (k - before[None, :]) * owners + ids[None, :]
    return jnp.sum(jnp.where(mine, spot, 0), axis=1, dtype=jnp.int32)


def work_plan(row, per):
    readers = row.shape[0]
    ids = jnp.arange(readers, dtype=jnp.int32)
    place = jnp.arange(2 * readers, dtype=jnp.int32)[:, None]
    start = jnp.int32(0)
    slots = jnp.zeros((2 * readers,), jnp.int32)
    live = jnp.zeros((2 * readers,), jnp.int32)
    for s in range(2):
        has = row > s
        rank = jnp.sum(jnp.where((ids[None, :] < ids[:, None]) & has[None, :], 1, 0), axis=1)
        hit = has[None, :] & (start + rank[None, :] == place)
        slots += jnp.sum(jnp.where(hit, s * readers + ids[None, :], 0), axis=1, dtype=jnp.int32)
        live += jnp.sum(hit, axis=1, dtype=jnp.int32)
        start = start + (jnp.sum(has, dtype=jnp.int32) + per - 1) // per * per
    return slots, live, jnp.maximum(start // per, 1).reshape(1)


def on_device(features, out_grad, pair_count, sample_grid, first_kernel, second_kernel):
    tiles, lines = lax.axis_size("tile"), lax.axis_size("group")
    own = lax.axis_index("tile")
    counts = pair_count[0]
    upstream = out_grad[0]
    regions = upstream.shape[0]
    column = lax.dynamic_index_in_dim(counts, own, 1, keepdims=False)
    row = lax.dynamic_index_in_dim(counts, own, 0, keepdims=False)

    packed = pack_upstream(send_plan(column, regions), upstream, 2 * tiles)
    packed = packed.reshape(2, tiles, PACK, CH)
    arrived = lax.all_to_all(packed, "tile", split_axis=1, concat_axis=1, tiled=True)
    arrived = arrived.reshape(2 * tiles, PACK, CH)

    grid = jnp.swapaxes(sample_grid[0, 0], 0, 1).reshape(2 * tiles, 4, RES)
    row_at = 16 * grid[:, 0, 0:2] + grid[:, 1, 0:2]
    col_at = 16 * grid[:, 2, 0:2] + grid[:, 3, 0:2]
    geo = jnp.stack(
        [row_at[:, 0], row_at[:, 1] - row_at[:, 0], col_at[:, 0], col_at[:, 1] - col_at[:, 0]],
        axis=1,
    ).reshape(-1)
    slots, live, steps = work_plan(row, PER)
    kept = forward(
        steps, slots, geo, features[0],
        first_kernel.reshape(3, WIDE, CH), second_kernel.reshape(3, WIDE, CH),
    )
    scale = 1.0 / math.sqrt(lines * tiles * regions * RES * RES)
    tile_grad, first_part, second_part = backward(
        steps, slots, live, geo, kept, arrived, turned(first_kernel), turned(second_kernel), scale
    )
    parts = jnp.stack([first_part.reshape(9 * CH, CH), second_part.reshape(9 * CH, CH)])
    sums = reduce_everywhere(parts, tiles, lines).astype(F32).reshape(2, 3, 3, CH, CH)
    return tile_grad[None], sums[0], sums[1]


def solution(mesh):
    return jax.shard_map(
        on_device,
        mesh=mesh,
        in_specs=(
            P("group", "tile", None, None),
            P("group", "tile", None, None, None),
            P("group", None, None),
            P("group", "tile", None, None, None, None),
            P(),
            P(),
        ),
        out_specs=(P("group", "tile", None, None), P(), P()),
        check_vma=False,
    )
```

time: 988 us -> 289 us (0.29); the launches traced: 975 us -> 289 us
  other arithmetic: 288 us -> 6.71 us
  local copies, waits for them, and re-layouts: 247 us -> 25 us
  waiting for transfers between devices: 247 us -> 42.4 us
  Pallas kernels: 0 us -> 203 us
  matrix products: 158 us -> 0 us
  between operations: 14.6 us -> 2.1 us
  starting transfers between devices: 19.9 us -> 9.61 us
    scatter-add x32 -> x0, other arithmetic: 251 us -> none  [the longest x8 94.8 us: spread_one_block(): running_sum = running_sum.at[flat_rows].add(lower_terms)]
    pallas_call x0 -> x4, Pallas kernels: none -> 203 us  [the longest x1 120 us: reduce_everywhere(): pl.pallas_call(functools.partial(reduce_kernel, planes, lines), in_specs=...]
    psum x1 -> x0, waiting for transfers between devices: 188 us -> none  [on_device(): lax.psum((first_raw, second_raw), ('tile', 'group'))]
    dot_general x22 -> x0, matrix products: 158 us -> none  [the longest x8 40.2 us: spread_one_block(): jnp.einsum('sqx,spqc->spxc', col_part, grad_part, preferred_element_type=...]
    gather x18 -> x0, local copies, waits for them, and re-layouts: 53.3 us -> none  [the longest x8 26.2 us: sample_one_block(): upper_taken = jnp.take(tile_image, low_part + 1, axis=0).astype(jnp.float32)]
    reshape x13 -> x3, local copies, waits for them, and re-layouts: 56.3 us -> 6.81 us  [the longest x1 6.05 us: on_device(): packed = packed.reshape(2, tiles, PACK, CH)]
    concatenate x10 -> x0, local copies, waits for them, and re-layouts: 39.8 us -> none  [unfold(): jnp.concatenate(pieces, axis=-1)]
    unnamed x52 -> x7, local copies, waits for them, and re-layouts: 36.6 us -> 3.8 us
  transfers between devices with their start and end apart: 3 -> 1, of which waited for: 2 -> 1; matrix products, arithmetic and copies ran while one was open for 5% -> 2% of each run, Pallas kernels for 0% -> 9%
where the time goes in v1:
time: 289 us
  Pallas kernels  203 us (70%)
  waiting for transfers between devices  42.4 us (15%)
  local copies, waits for them, and re-layouts  25 us (9%)
  starting transfers between devices  9.61 us (3%)
  other arithmetic  6.71 us (2%)
    pallas_call x1, Pallas kernels, reduce_everywhere(): pl.pallas_call(functools.partial(reduce_kernel, planes, lines), in_specs=...  120 us
    pallas_call x1, Pallas kernels, backward(): pl.pallas_call(functools.partial(backward_kernel, scale=scale), grid_spec...  52.3 us
    all_to_all x1, waiting for transfers between devices, on_device(): lax.all_to_all(packed, 'tile', split_axis=1, concat_axis=1, tiled=True)  42.4 us
    pallas_call x1, Pallas kernels, forward(): pl.pallas_call(forward_kernel, grid_spec=pltpu.PrefetchScalarGridSpec(num...  25.8 us
    all_to_all x1, starting transfers between devices, on_device(): lax.all_to_all(packed, 'tile', split_axis=1, concat_axis=1, tiled=True)  9.61 us
    reshape x1, local copies, waits for them, and re-layouts, on_device(): packed = packed.reshape(2, tiles, PACK, CH)  6.05 us
    all_to_all x1, local copies, waits for them, and re-layouts, on_device(): lax.all_to_all(packed, 'tile', split_axis=1, concat_axis=1, tiled=True)  5.99 us
  transfers between devices with their start and end apart: 1, of which 1 were waited for; matrix products, arithmetic and copies ran while one was open for 2% of the time, Pallas kernels for 9%

profile of v1, /device:TPU:1, one launch (start us, length us, event | category | flops | bytes accessed | tf_op | source)
XLA Modules:
  0.0 288.6 jit_solution(16460043029147214298)
XLA Ops:
  0.6 0.9 dynamic-slice_reduce_fusion
  1.5 0.1 select_reduce_fusion
  1.7 0.6 select_reduce_fusion.5.place_ref
  2.3 3.8 %copy.32 = bf16[1,22,14,14,256]{4,3,2,1,0:T(8,128)(2,1)} copy(bf16[1,22,14,14,256]{4,1,3,2,0:T(8,128)(2,1)} %param.7) | data formatting | bytes 4415488 | tf_op args[1]
  6.1 4.2 %shard_map.86 = bf16[64,200,256]{2,1,0:T(8,128)(2,1)} custom-call(s32[22]{0:T(128)} %select_reduce_fusion.5.place_ref, bf16[22,14,14,256]{3,2,1,0:T(8,128)(2,1)} %bitcast.36), custom_call_target="tpu_custom_call" | custom-call | tf_op jit(solution)/shard_map/pallas_call | solution.py:55
  10.3 6.1 %copy.27 = bf16[2,32,200,256]{3,2,0,1:T(8,128)(2,1)} copy(bf16[2,32,200,256]{3,2,1,0:T(8,128)(2,1)} %bitcast.35) | data formatting | bytes 13107200 | tf_op jit(solution)/shard_map/reshape | solution.py:477
  16.4 9.6 %all-to-all-start = ((bf16[2,32,200,256]{3,2,0,1:T(8,128)(2,1)}), bf16[2,32,200,256]{3,2,0,1:T(8,128)(2,1)}, u32[]{:S(2)}, u32[]{:S(2)}) async-start(bf16[2,32,200,256]{3,2,0,1:T(8,128)(2,1)} %copy.27), calls=%async_computation | async-start | bytes 13107200 | tf_op jit(solution)/shard_map/all_to_all | solution.py:478
  26.0 1.3 convert_reduce_fusion.2
  28.7 0.1 reshape.83
  29.0 0.6 reshape.84.refs_1_.geo_ref
  29.7 1.5 copy.29
  31.3 1.5 copy.30
  32.9 0.1 select_reduce_fusion.2
  33.0 0.1 select_reduce_fusion.4
  33.1 0.1 convert_reduce_fusion
  33.2 0.5 add.82.live_ref
  33.7 0.5 add.81.refs_0_.list_ref
  34.2 25.8 %shard_map.85.kept_ref = bf16[64,4,224,256]{3,2,1,0:T(8,128)(2,1)} custom-call(s32[1]{0:T(128)} %bitcast.2.steps_ref, s32[64]{0:T(128)} %add.81.refs_0_.list_ref, s32[256]{0:T(256)} %reshape.84.refs_1_.geo_ref, bf16[64,32,256]{2,1,0:T(8,128)(2,1)} %bitcast.45, bf16[3,768,256]{2,1,0:T(8,128)(2,1)} %bitcast.37, bf16[3,768,256]{2,1,0:T(8,128)(2,1)} %bitcast.38), custom_call_target="tpu_custom_call" | custom-call | tf_op jit(solution)/shard_map/pallas_call | solution.py:164
  60.0 42.4 %all-to-all-done = bf16[2,32,200,256]{3,2,0,1:T(8,128)(2,1)} async-done(((bf16[2,32,200,256]{3,2,0,1:T(8,128)(2,1)}), bf16[2,32,200,256]{3,2,0,1:T(8,128)(2,1)}, u32[]{:S(2)}, u32[]{:S(2)}) %all-to-all-start) | async-done | bytes 6553632 | tf_op jit(solution)/shard_map/all_to_all | solution.py:478
  102.5 6.0 %copy.28 = bf16[2,32,200,256]{3,2,1,0:T(8,128)(2,1)} copy(bf16[2,32,200,256]{3,2,0,1:T(8,128)(2,1)} %all-to-all-done) | data formatting | bytes 13107200 | tf_op jit(solution)/shard_map/all_to_all | solution.py:478
  108.4 52.3 %shard_map.87 = (bf16[64,32,256]{2,1,0:T(8,128)(2,1)}, bf16[3,3,256,256]{3,2,1,0:T(8,128)(2,1)}, bf16[3,3,256,256]{3,2,1,0:T(8,128)(2,1)}) custom-call(s32[1]{0:T(128)} %bitcast.2.steps_ref, s32[64]{0:T(128)} %add.81.refs_0_.list_ref, s32[64]{0:T(128)} %add.82.live_ref, s32[256]{0:T(256)} %reshape.84.refs_1_.geo_ref, ...), custom_call_target="tpu_custom_call" | custom-call | tf_op jit(solution)/shard_map/pallas_call | solution.py:272
  160.8 3.2 %pad_maximum_fusion.mine_ref = bf16[2,2304,256]{2,1,0:T(8,128)(2,1)} fusion(bf16[1,2304,256]{2,1,0:T(8,128)(2,1)} %bitcast.44, bf16[1,2304,256]{2,1,0:T(8,128)(2,1)} %bitcast.43), kind=kLoop, calls=%fused_computation.1 | loop fusion | flops 1179648 | bytes 4718592 | tf_op jit(solution)/shard_map/stack | solution.py:497
  164.0 120.4 %shard_map.88 = bf16[2,2304,256]{2,1,0:T(8,128)(2,1)} custom-call(bf16[2,2304,256]{2,1,0:T(8,128)(2,1)} %pad_maximum_fusion.mine_ref), custom_call_target="tpu_custom_call" | custom-call | tf_op jit(solution)/shard_map/pallas_call | solution.py:416
  284.4 4.2 %fusion.5 = (f32[1,2304,256]{2,1,0:T(8,128)}, f32[1,2304,256]{2,1,0:T(8,128)}) fusion(bf16[2,2304,256]{2,1,0:T(8,128)(2,1)} %shard_map.88), kind=kLoop, calls=%fused_computation.37 | loop fusion | bytes 9437184 | tf_op jit(solution)/shard_map/slice | solution.py:499
  (16 shorter events, 0.3 us)
Async XLA Ops:
  16.3 12.3 %copy-start.2 = (s32[1,1,32,2,4,14]{2,4,5,3,1,0:T(4,128)S(1)}, s32[1,1,32,2,4,14]{2,4,5,3,1,0:T(4,128)}, u32[]{:S(2)}) copy-start(s32[1,1,32,2,4,14]{2,4,5,3,1,0:T(4,128)} %param.9) | copy-start | bytes 43012
  16.4 13.3 %copy-start = (bf16[3,3,256,256]{3,2,1,0:T(8,128)(2,1)S(1)}, bf16[3,3,256,256]{3,2,1,0:T(8,128)(2,1)}, u32[]{:S(2)}) copy-start(bf16[3,3,256,256]{3,2,1,0:T(8,128)(2,1)} %param.10) | copy-start | bytes 3538948
  16.4 86.1 %all-to-all-start = ((bf16[2,32,200,256]{3,2,0,1:T(8,128)(2,1)}), bf16[2,32,200,256]{3,2,0,1:T(8,128)(2,1)}, u32[]{:S(2)}, u32[]{:S(2)}) async-start(bf16[2,32,200,256]{3,2,0,1:T(8,128)(2,1)} %copy.27), calls=%async_computation | async-start | bytes 13107200 | tf_op jit(solution)/shard_map/all_to_all | solution.py:478
  29.6 1.6 copy-start.1

commit v2 on v1

v2 whole, which is shorter than its diff:
```python
import functools
import math

import jax
import jax.numpy as jnp
from jax import lax
from jax.experimental import pallas as pl
from jax.experimental.pallas import tpu as pltpu
from jax.sharding import PartitionSpec as P

BF = jnp.bfloat16
F32 = jnp.float32
MESH = pl.DeviceIdType.MESH
RES = 14
PITCH = 16
FLAT = RES * PITCH
PACK = 200
CH = 256
WIDE = 3 * CH
TH = 64
TW = 32
VMEM = 60 * 1024 * 1024


def iota(shape, dim):
    return lax.broadcasted_iota(jnp.int32, shape, dim)


def dot(a, b):
    return jnp.dot(a, b, preferred_element_type=F32)


def packed_place(col):
    return jnp.where((col & 15) < RES, (col >> 4) * RES + (col & 15), -1)


def pack_kernel(slot_ref, owner_ref, grad_ref, out_zero, out_one, padded, packed, sems):
    regions = grad_ref.shape[0]
    padded[...] = jnp.zeros_like(padded)
    perm = (iota((PACK, FLAT), 0) == packed_place(iota((PACK, FLAT), 1))).astype(F32).astype(BF)

    def copy(k, out_ref):
        return pltpu.make_async_copy(packed.at[k], out_ref.at[owner_ref[k]], sems.at[k])

    for k in range(regions):
        padded[k % 4, :, 0:RES, :] = grad_ref[k]
        packed[k] = dot(perm, padded[k % 4].reshape(FLAT, CH)).astype(BF)
        for s, out_ref in enumerate((out_zero, out_one)):
            pl.when(slot_ref[k] == s)(copy(k, out_ref).start)
    for k in range(regions):
        copy(k, out_zero).wait()


def pack_upstream(plan, upstream, owners):
    regions = upstream.shape[0]
    return pl.pallas_call(
        pack_kernel,
        grid_spec=pltpu.PrefetchScalarGridSpec(
            num_scalar_prefetch=2,
            grid=(1,),
            in_specs=[pl.BlockSpec(upstream.shape, lambda i, *_: (0, 0, 0, 0))],
            out_specs=[pl.BlockSpec(memory_space=pl.ANY)] * 2,
            scratch_shapes=[
                pltpu.VMEM((4, RES, PITCH, CH), BF),
                pltpu.VMEM((regions, PACK, CH), BF),
                pltpu.SemaphoreType.DMA((regions,)),
            ],
        ),
        out_shape=[jax.ShapeDtypeStruct((owners, PACK, CH), BF)] * 2,
        compiler_params=pltpu.CompilerParams(vmem_limit_bytes=VMEM),
    )(*plan, upstream)


def put_shifted(ref, r, value):
    ref[r, PITCH : PITCH + FLAT, 0:CH] = pltpu.roll(value, 1, 0).astype(BF)
    ref[r, PITCH : PITCH + FLAT, CH : 2 * CH] = value.astype(BF)
    ref[r, PITCH : PITCH + FLAT, 2 * CH : WIDE] = pltpu.roll(value, FLAT - 1, 0).astype(BF)


def clear_edges(ref):
    edge = jnp.zeros((ref.shape[0], PITCH, WIDE), BF)
    ref[:, 0:PITCH, :] = edge
    ref[:, PITCH + FLAT : 2 * PITCH + FLAT, :] = edge


def taps(ref, r):
    return jnp.concatenate([ref[r, PITCH * a : PITCH * a + FLAT, :] for a in range(3)], axis=1)


def conv(ref, r, kernel_ref):
    return dot(taps(ref, r), kernel_ref[...].reshape(9 * CH, CH))


def conv_back(ref, r, kernel_ref):
    turned = jnp.concatenate([kernel_ref[8 - n] for n in range(9)], axis=1)
    return lax.dot_general(
        taps(ref, r), turned, (((1,), (1,)), ((), ())), preferred_element_type=F32
    )


def sampled_block(geo_ref, slot, tile_ref):
    row0, row_step = geo_ref[slot * 4], geo_ref[slot * 4 + 1]
    col0, col_step = geo_ref[slot * 4 + 2], geo_ref[slot * 4 + 3]
    lane, sub = iota((PITCH, CH), 1), iota((PITCH, CH), 0)
    reach = 16 - jnp.abs(16 * (lane & 31) - (col0 + col_step * sub))
    col_weight = jnp.where(sub < RES, jnp.maximum(reach, 0), 0).astype(F32)
    lower = (lane & 32) == 0
    owner = lane >> 6
    pieces = []
    for first in range(0, RES, 4):
        members = range(first, min(first + 4, RES))
        weights, rows = [], []
        for p in members:
            place = row0 + row_step * p
            low = place >> 4
            share = (place & 15).astype(F32) * (1.0 / 256.0)
            row_weight = jnp.where(lower, 1.0 / 16.0 - share, share)
            weights.append(jnp.where(owner == p - first, row_weight * col_weight, 0.0).astype(BF))
            rows.append(tile_ref[pl.ds(low, 2)].reshape(2 * TW, CH))
        depth = 64 * len(rows)
        left = jnp.concatenate(weights, axis=0)[:, 0:depth]
        pieces.append(dot(left, jnp.concatenate(rows, axis=0)))
    return jnp.concatenate(pieces, axis=0)


def sigmoid(v):
    return 0.5 * jnp.tanh(0.5 * v) + 0.5


def forward_kernel(steps_ref, *refs):
    wide_in, wide_hid = refs[-2:]

    @pl.when(pl.program_id(0) == 0)
    def _():
        clear_edges(wide_in)
        clear_edges(wide_hid)

    pl.when(pl.program_id(0) < steps_ref[0])(functools.partial(forward_step, *refs))


def forward_step(list_ref, geo_ref, tile_ref, first_ref, second_ref, out_ref, wide_in, wide_hid):
    step = pl.program_id(0)
    per = out_ref.shape[0]
    inside = (iota((FLAT, CH), 0) & 15) < RES
    for r in range(per):
        slot = list_ref[step * per + r]
        block = sampled_block(geo_ref, slot, tile_ref)
        put_shifted(wide_in, r, block)
        out_ref[r, 0] = block.astype(BF)
    for r in range(per):
        pre = conv(wide_in, r, first_ref)
        gate = sigmoid(pre)
        hidden = jnp.where(inside, pre * gate, 0.0)
        put_shifted(wide_hid, r, hidden)
        out_ref[r, 1] = hidden.astype(BF)
        out_ref[r, 2] = jnp.where(inside, gate * (1.0 + pre * (1.0 - gate)), 0.0).astype(BF)
    for r in range(per):
        pre = conv(wide_hid, r, second_ref)
        gate = sigmoid(pre)
        out_ref[r, 3] = (gate * (1.0 + pre * (1.0 - gate))).astype(BF)


PER = 4


def held(step, steps_ref):
    return jnp.minimum(step, steps_ref[0] - 1)


def forward(steps, slots, geo, tile, first, second):
    count = slots.shape[0]
    whole = lambda *shape: pl.BlockSpec(shape, lambda i, *_: (0,) * len(shape))
    return pl.pallas_call(
        forward_kernel,
        grid_spec=pltpu.PrefetchScalarGridSpec(
            num_scalar_prefetch=3,
            grid=(count // PER,),
            in_specs=[whole(TH, TW, CH), whole(9, CH, CH), whole(9, CH, CH)],
            out_specs=pl.BlockSpec(
                (PER, 4, FLAT, CH), lambda i, n, *_: (held(i, n), 0, 0, 0)
            ),
            scratch_shapes=[
                pltpu.VMEM((PER, FLAT + 2 * PITCH, WIDE), BF),
                pltpu.VMEM((PER, FLAT + 2 * PITCH, WIDE), BF),
            ],
        ),
        out_shape=jax.ShapeDtypeStruct((count, 4, FLAT, CH), BF),
        compiler_params=pltpu.CompilerParams(vmem_limit_bytes=VMEM),
    )(steps, slots, geo, tile, first, second)


def spread(geo_ref, slots, backs, grad_ref):
    up, along = iota((CH, 128), 0), iota((CH, 128), 1)
    same = ((along & 15) < RES) & ((up >> 5) == (along >> 4))
    weights = []
    for slot in slots:
        col0, col_step = geo_ref[slot * 4 + 2], geo_ref[slot * 4 + 3]
        reach = 16 - jnp.abs(16 * (up & 31) - (col0 + col_step * (along & 15)))
        weight = jnp.where(same, jnp.maximum(reach, 0), 0).astype(F32) * (1.0 / 16.0)
        weights.append(weight.astype(BF))
    for first in (0, 8):
        members = min(8, RES - first)
        stripes = [
            dot(
                weight[0 : members * TW, 0 : members * PITCH],
                back[first * PITCH : (first + members) * PITCH],
            )
            for weight, back in zip(weights, backs)
        ]
        for k in range(members):
            for slot, each in zip(slots, stripes):
                place = geo_ref[slot * 4] + geo_ref[slot * 4 + 1] * (first + k)
                low = place >> 4
                share = (place & 15).astype(F32) * (1.0 / 16.0)
                stripe = each[k * TW : (k + 1) * TW]
                upper = share * stripe
                pair = jnp.concatenate([(stripe - upper)[None], upper[None]], axis=0)
                grad_ref[pl.ds(low, 2)] = grad_ref[pl.ds(low, 2)] + pair


def backward_step(at, list_ref, live_ref, geo_ref, kept_ref, ups, first_ref, second_ref, scratch):
    wide_two, wide_one, first_acc, second_acc, tile_acc = scratch
    per = kept_ref.shape[0]
    unpack = (iota((FLAT, PACK), 1) == packed_place(iota((FLAT, PACK), 0))).astype(F32).astype(BF)
    for r, up in enumerate(ups):
        packed = jnp.where(live_ref[at + r] > 0, up[0], jnp.zeros_like(up[0]))
        put_shifted(wide_two, r, dot(unpack, packed) * kept_ref[r, 3].astype(F32))
    kernel_sums(kept_ref, 1, wide_two, second_acc)
    for r in range(per):
        hidden_back = conv_back(wide_two, r, second_ref)
        put_shifted(wide_one, r, hidden_back * kept_ref[r, 2].astype(F32))
    kernel_sums(kept_ref, 0, wide_one, first_acc)
    backs = [conv_back(wide_one, r, first_ref).astype(BF) for r in range(per)]
    spread(geo_ref, [list_ref[at + r] for r in range(per)], backs, tile_acc)


def kernel_sums(kept_ref, which, wide, acc):
    per = kept_ref.shape[0]
    values = kept_ref[:, which].reshape(per * FLAT, CH)
    for a in range(3):
        acc[a] += lax.dot_general(
            values, wide[:, PITCH * a : PITCH * a + FLAT, :].reshape(per * FLAT, WIDE),
            (((0,), (0,)), ((), ())), preferred_element_type=F32,
        )


def backward_kernel(begun, scale, steps_ref, list_ref, live_ref, geo_ref, kept_ref, *refs):
    ups, refs = refs[:PER], refs[PER:]
    first_ref, second_ref, refs = refs[0], refs[1], refs[2:]
    sums, refs = (refs[:3], refs[3:]) if begun else (None, refs)
    scratch = refs[-5:] if begun else refs[3:5] + refs[:3]
    wide_two, wide_one, first_acc, second_acc, tile_acc = scratch
    step = pl.program_id(0)

    @pl.when(step == 0)
    def _():
        clear_edges(wide_two)
        clear_edges(wide_one)
        first_acc[...] = jnp.zeros_like(first_acc)
        second_acc[...] = jnp.zeros_like(second_acc)
        tile_acc[...] = jnp.zeros_like(tile_acc)

    @pl.when(step < steps_ref[0])
    def _():
        at = (steps_ref[1] + step) * PER
        backward_step(at, list_ref, live_ref, geo_ref, kept_ref, ups, first_ref, second_ref, scratch)

    if begun:

        @pl.when(step == pl.num_programs(0) - 1)
        def _():
            tile_out, kernels_out = refs[:2]
            tile_out[...] = (tile_acc[...] + sums[2][...]).astype(BF)
            for n in range(9):
                row, cols = (8 - n) // 3, slice((8 - n) % 3 * CH, ((8 - n) % 3 + 1) * CH)
                for w, acc in enumerate((first_acc, second_acc)):
                    total = acc[row, :, cols] + sums[w][row, :, cols]
                    kernels_out[w, n * CH : (n + 1) * CH] = (total * scale).astype(BF)


def backward(slot, plan, geo, kept, arrived, first, second, sums, scale):
    steps, slots, live = plan
    readers = arrived.shape[0]
    begun = sums is not None
    whole = lambda *shape: pl.BlockSpec(shape, lambda i, *_: (0,) * len(shape))
    last = slots.shape[0] // PER - 1

    def group(i, n):
        return jnp.clip(n[1] + jnp.minimum(i, n[0] - 1), 0, last)

    def from_reader(j):
        def block(i, n, s, *_):
            return jnp.clip(s[PER * group(i, n) + j] - slot * readers, 0, readers - 1), 0, 0

        return pl.BlockSpec((1, PACK, CH), block)

    totals = [(3, CH, WIDE), (3, CH, WIDE), (TH, TW, CH)]
    wide = [pltpu.VMEM((PER, FLAT + 2 * PITCH, WIDE), BF)] * 2
    if begun:
        outs = [jax.ShapeDtypeStruct((TH, TW, CH), BF), jax.ShapeDtypeStruct((2, 9 * CH, CH), BF)]
        scratch = wide + [pltpu.VMEM(t, F32) for t in totals]
    else:
        outs = [jax.ShapeDtypeStruct(t, F32) for t in totals]
        scratch = wide
    return pl.pallas_call(
        functools.partial(backward_kernel, begun, scale),
        grid_spec=pltpu.PrefetchScalarGridSpec(
            num_scalar_prefetch=4,
            grid=(readers // PER,),
            in_specs=[
                pl.BlockSpec((PER, 4, FLAT, CH), lambda i, n, *_: (group(i, n), 0, 0, 0)),
                *[from_reader(j) for j in range(PER)],
                whole(9, CH, CH),
                whole(9, CH, CH),
                *([whole(*t) for t in totals] if begun else []),
            ],
            out_specs=[whole(*o.shape) for o in outs],
            scratch_shapes=scratch,
        ),
        out_shape=outs,
        compiler_params=pltpu.CompilerParams(vmem_limit_bytes=VMEM),
    )(steps, slots, live, geo, kept, *[arrived] * PER, first, second, *(sums or ()))


SIDE = 4
ORDERS = ((0, 1, 2), (1, 2, 0), (2, 0, 1))


def reduce_kernel(mine_ref, out_ref, pair_in, half, in_one, held_one, in_two, held_two, in_three, sems_s, sems_r):
    tile, line = lax.axis_index("tile"), lax.axis_index("group")
    core, x, z = tile & 1, (tile >> 1) & 3, tile >> 3
    coords = (z, x, line)
    third = mine_ref.shape[1] // 3
    quarter, small = third // SIDE, third // SIDE // SIDE

    def peer(axis, k):
        to = (coords[axis] + k) & (SIDE - 1)
        if axis == 0:
            return {"tile": to * 8 + x * 2 + core}
        if axis == 1:
            return {"tile": z * 8 + to * 2 + core}
        return {"group": to}

    other = {"tile": tile + 1 - 2 * core}

    def rows(start, size):
        return pl.ds(pl.multiple_of(start, 16), size)

    def remote(source, target, sem, device):
        return pltpu.make_async_remote_copy(
            source, target, sems_s.at[sem], sems_r.at[sem], device_id=device, device_id_type=MESH
        )

    barrier = pltpu.get_barrier_semaphore()
    pl.semaphore_signal(barrier, inc=1, device_id=other, device_id_type=MESH)
    for axis in range(3):
        for k in range(1, SIDE):
            pl.semaphore_signal(barrier, inc=1, device_id=peer(axis, k), device_id_type=MESH)
    pl.semaphore_wait(barrier, 1 + 3 * (SIDE - 1))

    def sem(stage, part, k):
        return 6 + (stage * 3 + part) * 3 + k - 1

    def swap(part):
        at = slice(part * third, (part + 1) * third)
        return remote(mine_ref.at[1 - core, at], pair_in.at[at], part, other)

    def one(part, k):
        axis = ORDERS[part][0]
        to = (coords[axis] + k) & (SIDE - 1)
        source = half.at[rows(part * third + to * quarter, quarter)]
        return remote(source, in_one.at[part, k - 1], sem(0, part, k), peer(axis, k))

    def two(part, k):
        axis = ORDERS[part][1]
        to = (coords[axis] + k) & (SIDE - 1)
        source = held_one.at[part, rows(to * small, small)]
        return remote(source, in_two.at[part, k - 1], sem(1, part, k), peer(axis, k))

    def three(part, k):
        return remote(held_two.at[part], in_three.at[part, k - 1], sem(2, part, k), peer(ORDERS[part][2], k))

    def start_of(part, first, second):
        return part * third + first * quarter + second * small

    def back_two(part, k, sender):
        first, second = ORDERS[part][:2]
        at = rows(start_of(part, coords[first], sender), small)
        return remote(out_ref.at[core, at], out_ref.at[core, at], sem(3, part, k), peer(second, k))

    def back_one(part, k, sender):
        first = ORDERS[part][0]
        at = rows(part * third + sender * quarter, quarter)
        return remote(out_ref.at[core, at], out_ref.at[core, at], sem(4, part, k), peer(first, k))

    def give(part, of):
        at = slice(part * third, (part + 1) * third)
        return remote(out_ref.at[of, at], out_ref.at[of, at], 3 + part, other)

    shifts = range(1, SIDE)
    parts = range(3)
    for part in parts:
        swap(part).start()
    for part in parts:
        swap(part).wait()
        at = slice(part * third, (part + 1) * third)
        half[at] = (mine_ref[core, at].astype(F32) + pair_in[at].astype(F32)).astype(BF)
        for k in shifts:
            one(part, k).start()
    for part in parts:
        own = coords[ORDERS[part][0]]
        total = half[rows(part * third + own * quarter, quarter)].astype(F32)
        for k in shifts:
            one(part, k).wait()
            total += in_one[part, k - 1].astype(F32)
        held_one[part] = total.astype(BF)
        for k in shifts:
            two(part, k).start()
    for part in parts:
        own = coords[ORDERS[part][1]]
        total = held_one[part, rows(own * small, small)].astype(F32)
        for k in shifts:
            two(part, k).wait()
            total += in_two[part, k - 1].astype(F32)
        held_two[part] = total.astype(BF)
        for k in shifts:
            three(part, k).start()
    for part in parts:
        first, second, axis = ORDERS[part]
        terms = [held_two[part].astype(F32)]
        for k in shifts:
            three(part, k).wait()
            terms.append(in_three[part, k - 1].astype(F32))
        total = None
        for place in range(SIDE):
            back = (coords[axis] - place) & (SIDE - 1)
            term = terms[0]
            for k in shifts:
                term = jnp.where(back == k, terms[k], term)
            total = term if total is None else total + term
        out_ref[core, rows(start_of(part, coords[first], coords[second]), small)] = total.astype(BF)
        for k in shifts:
            back_two(part, k, coords[second]).start()
    for part in parts:
        first, second, axis = ORDERS[part]
        for k in shifts:
            back_two(part, k, coords[second]).wait_send()
            back_two(part, k, (coords[second] - k) & (SIDE - 1)).wait_recv()
        for k in shifts:
            back_one(part, k, coords[first]).start()
    for part in parts:
        first = ORDERS[part][0]
        for k in shifts:
            back_one(part, k, coords[first]).wait_send()
            back_one(part, k, (coords[first] - k) & (SIDE - 1)).wait_recv()
        give(part, core).start()
    for part in parts:
        give(part, core).wait_send()
        give(part, 1 - core).wait_recv()


def reduce_everywhere(mine):
    rows = mine.shape[1]
    third = rows // 3
    quarter, small = third // SIDE, third // SIDE // SIDE
    spec = pl.BlockSpec(memory_space=pltpu.VMEM)
    return pl.pallas_call(
        reduce_kernel,
        in_specs=[spec],
        out_specs=spec,
        out_shape=jax.ShapeDtypeStruct(mine.shape, BF),
        scratch_shapes=[
            pltpu.VMEM((rows, CH), BF),
            pltpu.VMEM((rows, CH), BF),
            pltpu.VMEM((3, SIDE - 1, quarter, CH), BF),
            pltpu.VMEM((3, quarter, CH), BF),
            pltpu.VMEM((3, SIDE - 1, small, CH), BF),
            pltpu.VMEM((3, small, CH), BF),
            pltpu.VMEM((3, SIDE - 1, small, CH), BF),
            pltpu.SemaphoreType.DMA((6 + 45,)),
            pltpu.SemaphoreType.DMA((6 + 45,)),
        ],
        compiler_params=pltpu.CompilerParams(
            collective_id=0, has_side_effects=True, vmem_limit_bytes=VMEM
        ),
    )(mine)


def send_plan(column, regions):
    owners = column.shape[0]
    ids = jnp.arange(owners, dtype=jnp.int32)
    before = jnp.sum(jnp.where(ids[None, :] < ids[:, None], column[None, :], 0), axis=1)
    k = jnp.arange(regions, dtype=jnp.int32)[:, None]
    mine = (before[None, :] <= k) & (k < (before + column)[None, :])
    slot = jnp.sum(jnp.where(mine, k - before[None, :], 0), axis=1, dtype=jnp.int32)
    owner = jnp.sum(jnp.where(mine, ids[None, :], 0), axis=1, dtype=jnp.int32)
    return slot, owner


def work_plan(row):
    readers = row.shape[0]
    ids = jnp.arange(readers, dtype=jnp.int32)
    place = jnp.arange(2 * readers, dtype=jnp.int32)[:, None]
    steps_zero = (jnp.sum(row > 0, dtype=jnp.int32) + PER - 1) // PER
    steps_one = (jnp.sum(row > 1, dtype=jnp.int32) + PER - 1) // PER
    slots, live = 0, 0
    for s, start in ((0, 0), (1, PER * steps_zero)):
        has = row > s
        rank = jnp.sum(jnp.where((ids[None, :] < ids[:, None]) & has[None, :], 1, 0), axis=1)
        hit = has[None, :] & (start + rank[None, :] == place)
        slots += jnp.sum(jnp.where(hit, s * readers + ids[None, :], 0), axis=1, dtype=jnp.int32)
        live += jnp.sum(hit, axis=1, dtype=jnp.int32)
    zero = jnp.stack([steps_zero, jnp.zeros_like(steps_zero)])
    one = jnp.stack([steps_one, steps_zero])
    return slots, live, jnp.maximum(steps_zero + steps_one, 1).reshape(1), zero, one


def exchange(blocks):
    return lax.all_to_all(blocks, "tile", split_axis=0, concat_axis=0, tiled=True)


def on_device(features, out_grad, pair_count, sample_grid, first_kernel, second_kernel):
    tiles, lines = lax.axis_size("tile"), lax.axis_size("group")
    own = lax.axis_index("tile")
    counts = pair_count[0]
    upstream = out_grad[0]
    regions = upstream.shape[0]
    column = lax.dynamic_index_in_dim(counts, own, 1, keepdims=False)
    row = lax.dynamic_index_in_dim(counts, own, 0, keepdims=False)

    packed = pack_upstream(send_plan(column, regions), upstream, tiles)
    arrived = [exchange(packed[0])]

    grid = jnp.swapaxes(sample_grid[0, 0], 0, 1).reshape(2 * tiles, 4, RES)
    row_at = 16 * grid[:, 0, 0:2] + grid[:, 1, 0:2]
    col_at = 16 * grid[:, 2, 0:2] + grid[:, 3, 0:2]
    geo = jnp.stack(
        [row_at[:, 0], row_at[:, 1] - row_at[:, 0], col_at[:, 0], col_at[:, 1] - col_at[:, 0]],
        axis=1,
    ).reshape(-1)
    slots, live, steps, zero, one = work_plan(row)
    first, second = first_kernel.reshape(9, CH, CH), second_kernel.reshape(9, CH, CH)
    kept = forward(steps, slots, geo, features[0], first, second)
    later, kept = lax.optimization_barrier((packed[1], kept))
    arrived.append(exchange(later))
    scale = 1.0 / math.sqrt(lines * tiles * regions * RES * RES)
    sums = backward(0, (zero, slots, live), geo, kept, arrived[0], first, second, None, scale)
    tile_grad, parts = backward(1, (one, slots, live), geo, kept, arrived[1], first, second, sums, scale)
    totals = reduce_everywhere(parts).astype(F32).reshape(2, 3, 3, CH, CH)
    return tile_grad[None], totals[0], totals[1]


def solution(mesh):
    return jax.shard_map(
        on_device,
        mesh=mesh,
        in_specs=(
            P("group", "tile", None, None),
            P("group", "tile", None, None, None),
            P("group", None, None),
            P("group", "tile", None, None, None, None),
            P(),
            P(),
        ),
        out_specs=(P("group", "tile", None, None), P(), P()),
        check_vma=False,
    )
```

time: 289 us -> 227 us (0.79)
  waiting for transfers between devices: 42.4 us -> 0.01 us
  local copies, waits for them, and re-layouts: 25 us -> 11.5 us
  Pallas kernels: 203 us -> 190 us
  starting transfers between devices: 9.61 us -> 18.2 us
    all_to_all x1 -> x2, waiting for transfers between devices: 42.4 us -> 0.01 us  [exchange(): lax.all_to_all(blocks, 'tile', split_axis=0, concat_axis=0, tiled=True)]
    pallas_call x2 -> x3, Pallas kernels: 173 us -> 142 us  [the longest x2 97.3 us: backward(): pl.pallas_call(functools.partial(backward_kernel, begun, scale), grid_spe...]
    pallas_call x1, Pallas kernels: 25.8 us -> 43.5 us  [forward(): pl.pallas_call(forward_kernel, grid_spec=pltpu.PrefetchScalarGridSpec(num...]
    all_to_all x1 -> x2, starting transfers between devices: 9.61 us -> 18.2 us  [exchange(): lax.all_to_all(blocks, 'tile', split_axis=0, concat_axis=0, tiled=True)]
    reshape x1 -> x0, local copies, waits for them, and re-layouts: 6.05 us -> none  [on_device(): packed = packed.reshape(2, tiles, PACK, CH)]
    all_to_all x1 -> x0, local copies, waits for them, and re-layouts: 5.99 us -> none  [on_device(): lax.all_to_all(packed, 'tile', split_axis=1, concat_axis=1, tiled=True)]
    transpose x4 -> x0, local copies, waits for them, and re-layouts: 3.23 us -> none  [turned(): return jnp.transpose(kernel[::-1, ::-1], (0, 1, 3, 2)).reshape(3, WIDE, CH)]
  transfers between devices with their start and end apart: 1 -> 2, of which waited for: 1 -> 0; matrix products, arithmetic and copies ran while one was open for 2% -> 2% of each run, Pallas kernels for 9% -> 44%
where the time goes in v2:
time: 227 us
  Pallas kernels  190 us (84%)
  starting transfers between devices  18.2 us (8%)
  local copies, waits for them, and re-layouts  11.5 us (5%)
  other arithmetic  4.82 us (2%)
    pallas_call x2, Pallas kernels, backward(): pl.pallas_call(functools.partial(backward_kernel, begun, scale), grid_spe...  97.3 us
    pallas_call x1, Pallas kernels, reduce_everywhere(): pl.pallas_call(reduce_kernel, in_specs=[spec], out_specs=spec, out_shape=...  45 us
    pallas_call x1, Pallas kernels, forward(): pl.pallas_call(forward_kernel, grid_spec=pltpu.PrefetchScalarGridSpec(num...  43.5 us
    all_to_all x2, starting transfers between devices, exchange(): lax.all_to_all(blocks, 'tile', split_axis=0, concat_axis=0, tiled=True)  18.2 us
    unnamed x5, local copies, waits for them, and re-layouts  5.44 us
  transfers between devices with their start and end apart: 2, of which 0 were waited for; matrix products, arithmetic and copies ran while one was open for 2% of the time, Pallas kernels for 44%

profile of v2, /device:TPU:1, one launch (start us, length us, event | category | flops | bytes accessed | tf_op | source)
XLA Modules:
  0.0 226.6 jit_solution(5930171334380271138)
XLA Ops:
  0.6 0.9 dynamic-slice_reduce_fusion
  1.5 0.1 select_reduce_fusion
  1.7 0.6 select_reduce_fusion.5
  2.3 3.7 %copy.17 = bf16[1,22,14,14,256]{4,3,2,1,0:T(8,128)(2,1)} copy(bf16[1,22,14,14,256]{4,1,3,2,0:T(8,128)(2,1)} %param.7) | data formatting | bytes 4415488 | tf_op args[1]
  6.0 4.2 %shard_map.85 = (bf16[32,200,256]{2,1,0:T(8,128)(2,1)}, bf16[32,200,256]{2,1,0:T(8,128)(2,1)}) custom-call(s32[22]{0:T(128)} %get-tuple-element.22.slot_ref, s32[22]{0:T(128)} %get-tuple-element.21.owner_ref, bf16[22,14,14,256]{3,2,1,0:T(8,128)(2,1)} %bitcast.31), custom_call_target="tpu_custom_call" | custom-call | tf_op jit(solution)/shard_map/pallas_call | solution.py:56
  10.3 9.5 %all-to-all-start.1 = ((bf16[32,200,256]{2,1,0:T(8,128)(2,1)}), bf16[32,200,256]{2,1,0:T(8,128)(2,1)S(1)}, u32[]{:S(2)}, u32[]{:S(2)}) async-start(bf16[32,200,256]{2,1,0:T(8,128)(2,1)} %get-tuple-element.15), calls=%async_computation.1 | async-start | bytes 6553600 | tf_op jit(solution)/shard_map/all_to_all | solution.py:519
  19.8 1.3 convert_reduce_fusion.3
  22.5 0.1 reshape.70
  22.7 0.1 copy.14
  22.8 0.7 reshape.71.refs_1_.geo_ref
  23.5 0.1 select_reduce_fusion.2
  23.6 0.1 select_reduce_fusion.4
  23.7 0.1 convert_reduce_fusion
  23.8 0.6 add.71.refs_0_.list_ref
  24.4 43.5 %shard_map.86.kept_ref = bf16[64,4,224,256]{3,2,1,0:T(8,128)(2,1)} custom-call(s32[1]{0:T(128)} %bitcast.9.steps_ref, s32[64]{0:T(128)} %add.71.refs_0_.list_ref, s32[256]{0:T(256)} %reshape.71.refs_1_.geo_ref, bf16[64,32,256]{2,1,0:T(8,128)(2,1)} %bitcast.34, bf16[9,256,256]{2,1,0:T(8,128)(2,1)} %bitcast.25, bf16[9,256,256]{2,1,0:T(8,128)(2,1)} %bitcast.28), custom_call_target="tpu_custom_call" | custom-call | tf_op jit(solution)/shard_map/pallas_call | solution.py:173
  67.9 1.7 copy-done
  69.7 8.7 %all-to-all-start = ((bf16[32,200,256]{2,1,0:T(8,128)(2,1)}), bf16[32,200,256]{2,1,0:T(8,128)(2,1)}, u32[]{:S(2)}, u32[]{:S(2)}) async-start(bf16[32,200,256]{2,1,0:T(8,128)(2,1)} %get-tuple-element.14), calls=%async_computation | async-start | bytes 6553600 | tf_op jit(solution)/shard_map/all_to_all | solution.py:519
  78.3 0.6 add.72.live_ref
  78.9 0.6 pad_add_fusion.1.steps_ref
  79.5 0.6 pad_add_fusion.2.steps_ref
  80.1 57.0 %shard_map.87 = (f32[3,256,768]{2,1,0:T(8,128)}, f32[3,256,768]{2,1,0:T(8,128)}, f32[64,32,256]{2,1,0:T(8,128)}) custom-call(s32[2]{0:T(128)} %pad_add_fusion.2.steps_ref, s32[64]{0:T(128)} %add.71.refs_0_.list_ref, s32[64]{0:T(128)} %add.72.live_ref, s32[256]{0:T(256)} %reshape.71.refs_1_.geo_ref, bf16[64,4,224,256]{3,2,1,0:T(8,128)(2,1)} %shard_map.86.kept_ref, ...), custom_call_target="tpu_custom_call" | custom-call | tf_op jit(solution)/shard_map/pallas_call | solution.py:305
  137.1 40.3 %shard_map.88 = (bf16[64,32,256]{2,1,0:T(8,128)(2,1)}, bf16[2,2304,256]{2,1,0:T(8,128)(2,1)}) custom-call(s32[2]{0:T(128)} %pad_add_fusion.1.steps_ref, s32[64]{0:T(128)} %add.71.refs_0_.list_ref, s32[64]{0:T(128)} %add.72.live_ref, s32[256]{0:T(256)} %reshape.71.refs_1_.geo_ref, bf16[64,4,224,256]{3,2,1,0:T(8,128)(2,1)} %shard_map.86.kept_ref, ...), custom_call_target="tpu_custom_call" | custom-call | tf_op jit(solution)/shard_map/pallas_call | solution.py:305
  177.4 45.0 %shard_map.89 = bf16[2,2304,256]{2,1,0:T(8,128)(2,1)} custom-call(bf16[2,2304,256]{2,1,0:T(8,128)(2,1)} %get-tuple-element.20.mine_ref), custom_call_target="tpu_custom_call" | custom-call | tf_op jit(solution)/shard_map/pallas_call | solution.py:467
  222.4 4.2 %fusion.5 = (f32[1,2304,256]{2,1,0:T(8,128)}, f32[1,2304,256]{2,1,0:T(8,128)}) fusion(bf16[2,2304,256]{2,1,0:T(8,128)(2,1)} %shard_map.89), kind=kLoop, calls=%fused_computation.37 | loop fusion | bytes 9437184 | tf_op jit(solution)/shard_map/slice | solution.py:550
  (12 shorter events, 0.1 us)
Async XLA Ops:
  10.3 12.2 %copy-start.1 = (s32[1,1,32,2,4,14]{2,4,5,3,1,0:T(4,128)S(1)}, s32[1,1,32,2,4,14]{2,4,5,3,1,0:T(4,128)}, u32[]{:S(2)}) copy-start(s32[1,1,32,2,4,14]{2,4,5,3,1,0:T(4,128)} %param.9) | copy-start | bytes 43012
  10.3 57.7 %all-to-all-start.1 = ((bf16[32,200,256]{2,1,0:T(8,128)(2,1)}), bf16[32,200,256]{2,1,0:T(8,128)(2,1)S(1)}, u32[]{:S(2)}, u32[]{:S(2)}) async-start(bf16[32,200,256]{2,1,0:T(8,128)(2,1)} %get-tuple-element.15), calls=%async_computation.1 | async-start | bytes 6553600 | tf_op jit(solution)/shard_map/all_to_all | solution.py:519
  67.9 1.7 copy-start
  69.7 67.4 %all-to-all-start = ((bf16[32,200,256]{2,1,0:T(8,128)(2,1)}), bf16[32,200,256]{2,1,0:T(8,128)(2,1)}, u32[]{:S(2)}, u32[]{:S(2)}) async-start(bf16[32,200,256]{2,1,0:T(8,128)(2,1)} %get-tuple-element.14), calls=%async_computation | async-start | bytes 6553600 | tf_op jit(solution)/shard_map/all_to_all | solution.py:519

commit v3 on v2

--- a/solution.py
+++ b/solution.py
@@ -83,19 +83,13 @@
     ref[:, PITCH + FLAT : 2 * PITCH + FLAT, :] = edge
 
 
-def taps(ref, r):
-    return jnp.concatenate([ref[r, PITCH * a : PITCH * a + FLAT, :] for a in range(3)], axis=1)
-
-
-def conv(ref, r, kernel_ref):
-    return dot(taps(ref, r), kernel_ref[...].reshape(9 * CH, CH))
+def conv(ref, r, kernel_ref, a):
+    return dot(ref[r, PITCH * a : PITCH * a + FLAT, :], kernel_ref[3 * a : 3 * a + 3].reshape(WIDE, CH))
 
 
 def conv_back(ref, r, kernel_ref):
-    turned = jnp.concatenate([kernel_ref[8 - n] for n in range(9)], axis=1)
-    return lax.dot_general(
-        taps(ref, r), turned, (((1,), (1,)), ((), ())), preferred_element_type=F32
-    )
+    sides = [ref[r, PITCH * a : PITCH * a + FLAT, :] for a in range(3)]
+    return dot(jnp.concatenate(sides, axis=1), kernel_ref[...].reshape(9 * CH, CH))
 
 
 def sampled_block(geo_ref, slot, tile_ref):
@@ -142,22 +136,45 @@
     step = pl.program_id(0)
     per = out_ref.shape[0]
     inside = (iota((FLAT, CH), 0) & 15) < RES
-    for r in range(per):
-        slot = list_ref[step * per + r]
-        block = sampled_block(geo_ref, slot, tile_ref)
+
+    def sample(r):
+        block = sampled_block(geo_ref, list_ref[step * per + r], tile_ref)
         put_shifted(wide_in, r, block)
         out_ref[r, 0] = block.astype(BF)
-    for r in range(per):
-        pre = conv(wide_in, r, first_ref)
+
+    def hide(r, pre):
         gate = sigmoid(pre)
         hidden = jnp.where(inside, pre * gate, 0.0)
         put_shifted(wide_hid, r, hidden)
         out_ref[r, 1] = hidden.astype(BF)
-        out_ref[r, 2] = jnp.where(inside, gate * (1.0 + pre * (1.0 - gate)), 0.0).astype(BF)
-    for r in range(per):
-        pre = conv(wide_hid, r, second_ref)
+        out_ref[r, 2] = jnp.where(inside, gate + hidden * (1.0 - gate), 0.0).astype(BF)
+
+    def finish(r, pre):
         gate = sigmoid(pre)
         out_ref[r, 3] = (gate * (1.0 + pre * (1.0 - gate))).astype(BF)
+
+    sample(0)
+    held_pre = None
+    for r in range(per):
+        pre = conv(wide_in, r, first_ref, 0)
+        if r + 1 < per:
+            sample(r + 1)
+        pre += conv(wide_in, r, first_ref, 1)
+        if r:
+            hide(r - 1, held_pre)
+        pre += conv(wide_in, r, first_ref, 2)
+        held_pre = pre
+    last = held_pre
+    for r in range(per):
+        pre = conv(wide_hid, r, second_ref, 0)
+        if r == 0:
+            hide(per - 1, last)
+        else:
+            finish(r - 1, held_pre)
+        pre += conv(wide_hid, r, second_ref, 1)
+        pre += conv(wide_hid, r, second_ref, 2)
+        held_pre = pre
+    finish(per - 1, held_pre)
 
 
 PER = 4
@@ -189,59 +206,73 @@
     )(steps, slots, geo, tile, first, second)
 
 
-def spread(geo_ref, slots, backs, grad_ref):
+def spread(geo_ref, slot, back, grad_ref, half):
     up, along = iota((CH, 128), 0), iota((CH, 128), 1)
+    col0, col_step = geo_ref[slot * 4 + 2], geo_ref[slot * 4 + 3]
     same = ((along & 15) < RES) & ((up >> 5) == (along >> 4))
-    weights = []
-    for slot in slots:
-        col0, col_step = geo_ref[slot * 4 + 2], geo_ref[slot * 4 + 3]
-        reach = 16 - jnp.abs(16 * (up & 31) - (col0 + col_step * (along & 15)))
-        weight = jnp.where(same, jnp.maximum(reach, 0), 0).astype(F32) * (1.0 / 16.0)
-        weights.append(weight.astype(BF))
-    for first in (0, 8):
-        members = min(8, RES - first)
-        stripes = [
-            dot(
-                weight[0 : members * TW, 0 : members * PITCH],
-                back[first * PITCH : (first + members) * PITCH],
-            )
-            for weight, back in zip(weights, backs)
-        ]
-        for k in range(members):
-            for slot, each in zip(slots, stripes):
-                place = geo_ref[slot * 4] + geo_ref[slot * 4 + 1] * (first + k)
-                low = place >> 4
-                share = (place & 15).astype(F32) * (1.0 / 16.0)
-                stripe = each[k * TW : (k + 1) * TW]
-                upper = share * stripe
-                pair = jnp.concatenate([(stripe - upper)[None], upper[None]], axis=0)
-                grad_ref[pl.ds(low, 2)] = grad_ref[pl.ds(low, 2)] + pair
+    reach = 16 - jnp.abs(16 * (up & 31) - (col0 + col_step * (along & 15)))
+    weight = jnp.where(same, jnp.maximum(reach, 0), 0).astype(F32) * (1.0 / 16.0)
+    first = 8 * half
+    members = min(8, RES - first)
+    stripes = dot(
+        weight[0 : members * TW, 0 : members * PITCH].astype(BF),
+        back[first * PITCH : (first + members) * PITCH],
+    )
+    for k in range(members):
+        place = geo_ref[slot * 4] + geo_ref[slot * 4 + 1] * (first + k)
+        low = place >> 4
+        share = (place & 15).astype(F32) * (1.0 / 16.0)
+        stripe = stripes[k * TW : (k + 1) * TW]
+        upper = share * stripe
+        pair = jnp.concatenate([(stripe - upper)[None], upper[None]], axis=0)
+        grad_ref[pl.ds(low, 2)] = grad_ref[pl.ds(low, 2)] + pair
 
 
 def backward_step(at, list_ref, live_ref, geo_ref, kept_ref, ups, first_ref, second_ref, scratch):
     wide_two, wide_one, first_acc, second_acc, tile_acc = scratch
     per = kept_ref.shape[0]
     unpack = (iota((FLAT, PACK), 1) == packed_place(iota((FLAT, PACK), 0))).astype(F32).astype(BF)
-    for r, up in enumerate(ups):
-        packed = jnp.where(live_ref[at + r] > 0, up[0], jnp.zeros_like(up[0]))
+    def upstream(r):
+        packed = jnp.where(live_ref[at + r] > 0, ups[r][0], jnp.zeros_like(ups[r][0]))
         put_shifted(wide_two, r, dot(unpack, packed) * kept_ref[r, 3].astype(F32))
-    kernel_sums(kept_ref, 1, wide_two, second_acc)
+
+    def first_delta(r, hidden_back):
+        put_shifted(wide_one, r, hidden_back * kept_ref[r, 2].astype(F32))
+
+    def give_back(r, back, half):
+        spread(geo_ref, list_ref[at + r], back, tile_acc, half)
+
+    upstream(0)
+    upstream(1)
+    held = []
     for r in range(per):
-        hidden_back = conv_back(wide_two, r, second_ref)
-        put_shifted(wide_one, r, hidden_back * kept_ref[r, 2].astype(F32))
-    kernel_sums(kept_ref, 0, wide_one, first_acc)
-    backs = [conv_back(wide_one, r, first_ref).astype(BF) for r in range(per)]
-    spread(geo_ref, [list_ref[at + r] for r in range(per)], backs, tile_acc)
-
-
-def kernel_sums(kept_ref, which, wide, acc):
+        held.append(conv_back(wide_two, r, second_ref))
+        if r + 2 < per:
+            upstream(r + 2)
+        if r:
+            first_delta(r - 1, held[r - 1])
+    kernel_sums(kept_ref, 1, wide_two, second_acc, 0)
+    first_delta(per - 1, held[per - 1])
+    kernel_sums(kept_ref, 1, wide_two, second_acc, 1)
+    kernel_sums(kept_ref, 1, wide_two, second_acc, 2)
+    held = []
+    for r in range(per):
+        held.append(conv_back(wide_one, r, first_ref).astype(BF))
+    for a in range(3):
+        kernel_sums(kept_ref, 0, wide_one, first_acc, a)
+        give_back(a, held[a], 0)
+        give_back(a, held[a], 1)
+    give_back(3, held[3], 0)
+    give_back(3, held[3], 1)
+
+
+def kernel_sums(kept_ref, which, wide, acc, a):
     per = kept_ref.shape[0]
     values = kept_ref[:, which].reshape(per * FLAT, CH)
-    for a in range(3):
-        acc[a] += lax.dot_general(
-            values, wide[:, PITCH * a : PITCH * a + FLAT, :].reshape(per * FLAT, WIDE),
-            (((0,), (0,)), ((), ())), preferred_element_type=F32,
-        )
+    acc[a] += lax.dot_general(
+        values, wide[:, PITCH * a : PITCH * a + FLAT, :].reshape(per * FLAT, WIDE),
+        (((0,), (0,)), ((), ())), preferred_element_type=F32,
+    )
 
 
 def backward_kernel(begun, scale, steps_ref, list_ref, live_ref, geo_ref, kept_ref, *refs):
@@ -515,6 +546,10 @@
     return slots, live, jnp.maximum(steps_zero + steps_one, 1).reshape(1), zero, one
 
 
+def turned(kernel):
+    return jnp.transpose(kernel[::-1, ::-1], (0, 1, 3, 2)).reshape(9, CH, CH)
+
+
 def exchange(blocks):
     return lax.all_to_all(blocks, "tile", split_axis=0, concat_axis=0, tiled=True)
 
@@ -543,6 +578,7 @@
     kept = forward(steps, slots, geo, features[0], first, second)
     later, kept = lax.optimization_barrier((packed[1], kept))
     arrived.append(exchange(later))
+    first, second = turned(first_kernel), turned(second_kernel)
     scale = 1.0 / math.sqrt(lines * tiles * regions * RES * RES)
     sums = backward(0, (zero, slots, live), geo, kept, arrived[0], first, second, None, scale)
     tile_grad, parts = backward(1, (one, slots, live), geo, kept, arrived[1], first, second, sums, scale)

time: 227 us -> 228 us (level)
  Pallas kernels: 190 us -> 174 us
  starting transfers between devices: 18.2 us -> 27.8 us
  local copies, waits for them, and re-layouts: 11.5 us -> 16.1 us
  waiting for transfers between devices: 0.01 us -> 2.88 us
    pallas_call x2, Pallas kernels: 97.3 us -> 72.3 us  [backward(): pl.pallas_call(functools.partial(backward_kernel, begun, scale), grid_spe...]
    pallas_call x1, Pallas kernels: 45 us -> 64.4 us  [reduce_everywhere(): pl.pallas_call(reduce_kernel, in_specs=[spec], out_specs=spec, out_shape=...]
    pallas_call x1, Pallas kernels: 43.5 us -> 33.1 us  [forward(): pl.pallas_call(forward_kernel, grid_spec=pltpu.PrefetchScalarGridSpec(num...]
    all_to_all x2, starting transfers between devices: 18.2 us -> 27.8 us  [exchange(): lax.all_to_all(blocks, 'tile', split_axis=0, concat_axis=0, tiled=True)]
    transpose x0 -> x4, local copies, waits for them, and re-layouts: none -> 4.65 us  [turned(): return jnp.transpose(kernel[::-1, ::-1], (0, 1, 3, 2)).reshape(9, CH, CH)]
    all_to_all x2, waiting for transfers between devices: 0.01 us -> 2.88 us  [exchange(): lax.all_to_all(blocks, 'tile', split_axis=0, concat_axis=0, tiled=True)]
    unnamed x5 -> x7, local copies, waits for them, and re-layouts: 5.44 us -> 5.44 us
  transfers between devices with their start and end apart: 2 -> 2, of which waited for: 0 -> 1; matrix products, arithmetic and copies ran while one was open for 2% -> 4% of each run, Pallas kernels for 44% -> 37%
where the time goes in v3:
time: 228 us
  Pallas kernels  174 us (76%)
  starting transfers between devices  27.8 us (12%)
  local copies, waits for them, and re-layouts  16.1 us (7%)
  other arithmetic  4.81 us (2%)
  waiting for transfers between devices  2.88 us (1%)
    pallas_call x2, Pallas kernels, backward(): pl.pallas_call(functools.partial(backward_kernel, begun, scale), grid_spe...  72.3 us
    pallas_call x1, Pallas kernels, reduce_everywhere(): pl.pallas_call(reduce_kernel, in_specs=[spec], out_specs=spec, out_shape=...  64.4 us
    pallas_call x1, Pallas kernels, forward(): pl.pallas_call(forward_kernel, grid_spec=pltpu.PrefetchScalarGridSpec(num...  33.1 us
    all_to_all x2, starting transfers between devices, exchange(): lax.all_to_all(blocks, 'tile', split_axis=0, concat_axis=0, tiled=True)  27.8 us
    unnamed x7, local copies, waits for them, and re-layouts  5.44 us
    transpose x4, local copies, waits for them, and re-layouts, turned(): return jnp.transpose(kernel[::-1, ::-1], (0, 1, 3, 2)).reshape(9, CH, CH)  4.65 us
  transfers between devices with their start and end apart: 2, of which 1 were waited for; matrix products, arithmetic and copies ran while one was open for 4% of the time, Pallas kernels for 37%

profile of v3, /device:TPU:1, one launch (start us, length us, event | category | flops | bytes accessed | tf_op | source)
XLA Modules:
  0.0 227.8 jit_solution(2859236136009746281)
XLA Ops:
  0.6 0.9 dynamic-slice_reduce_fusion
  1.5 0.1 select_reduce_fusion
  1.7 0.6 select_reduce_fusion.5
  2.3 3.7 %copy.23 = bf16[1,22,14,14,256]{4,3,2,1,0:T(8,128)(2,1)} copy(bf16[1,22,14,14,256]{4,1,3,2,0:T(8,128)(2,1)} %param.7) | data formatting | bytes 4415488 | tf_op args[1]
  6.0 4.2 %shard_map.85 = (bf16[32,200,256]{2,1,0:T(8,128)(2,1)}, bf16[32,200,256]{2,1,0:T(8,128)(2,1)}) custom-call(s32[22]{0:T(128)} %get-tuple-element.22.slot_ref, s32[22]{0:T(128)} %get-tuple-element.21.owner_ref, bf16[22,14,14,256]{3,2,1,0:T(8,128)(2,1)} %bitcast.35), custom_call_target="tpu_custom_call" | custom-call | tf_op jit(solution)/shard_map/pallas_call | solution.py:56
  10.2 9.6 %all-to-all-start.1 = ((bf16[32,200,256]{2,1,0:T(8,128)(2,1)}), bf16[32,200,256]{2,1,0:T(8,128)(2,1)S(1)}, u32[]{:S(2)}, u32[]{:S(2)}) async-start(bf16[32,200,256]{2,1,0:T(8,128)(2,1)} %get-tuple-element.15), calls=%async_computation.1 | async-start | bytes 6553600 | tf_op jit(solution)/shard_map/all_to_all | solution.py:554
  19.8 1.3 convert_reduce_fusion.3
  22.8 0.6 reshape.77.refs_1_.geo_ref
  23.6 0.1 select_reduce_fusion.4
  23.8 0.5 add.71.refs_0_.list_ref
  24.3 33.1 %shard_map.86.kept_ref = bf16[64,4,224,256]{3,2,1,0:T(8,128)(2,1)} custom-call(s32[1]{0:T(128)} %bitcast.9.steps_ref, s32[64]{0:T(128)} %add.71.refs_0_.list_ref, s32[256]{0:T(256)} %reshape.77.refs_1_.geo_ref, bf16[64,32,256]{2,1,0:T(8,128)(2,1)} %bitcast.40, bf16[9,256,256]{2,1,0:T(8,128)(2,1)} %bitcast.36, bf16[9,256,256]{2,1,0:T(8,128)(2,1)} %bitcast.37), custom_call_target="tpu_custom_call" | custom-call | tf_op jit(solution)/shard_map/pallas_call | solution.py:190
  57.4 2.9 %all-to-all-done.1.refs_0_.refs_1_.refs_2_.refs_3_ = bf16[32,200,256]{2,1,0:T(8,128)(2,1)S(1)} async-done(((bf16[32,200,256]{2,1,0:T(8,128)(2,1)}), bf16[32,200,256]{2,1,0:T(8,128)(2,1)S(1)}, u32[]{:S(2)}, u32[]{:S(2)}) %all-to-all-start.1) | async-done | bytes 3276832 | tf_op jit(solution)/shard_map/all_to_all | solution.py:554
  60.3 1.7 copy-done
  62.0 18.3 %all-to-all-start = ((bf16[32,200,256]{2,1,0:T(8,128)(2,1)}), bf16[32,200,256]{2,1,0:T(8,128)(2,1)}, u32[]{:S(2)}, u32[]{:S(2)}) async-start(bf16[32,200,256]{2,1,0:T(8,128)(2,1)} %get-tuple-element.14), calls=%async_computation | async-start | bytes 6553600 | tf_op jit(solution)/shard_map/all_to_all | solution.py:554
  80.3 1.4 reverse_bitcast_fusion.1
  81.8 1.6 copy.20
  83.4 1.6 copy.21
  85.0 0.6 add.72.live_ref
  85.6 0.6 pad_add_fusion.1.steps_ref
  86.2 0.6 pad_add_fusion.2.steps_ref
  86.8 51.9 %shard_map.87 = (f32[3,256,768]{2,1,0:T(8,128)}, f32[3,256,768]{2,1,0:T(8,128)}, f32[64,32,256]{2,1,0:T(8,128)}) custom-call(s32[2]{0:T(128)} %pad_add_fusion.2.steps_ref, s32[64]{0:T(128)} %add.71.refs_0_.list_ref, s32[64]{0:T(128)} %add.72.live_ref, s32[256]{0:T(256)} %reshape.77.refs_1_.geo_ref, bf16[64,4,224,256]{3,2,1,0:T(8,128)(2,1)} %shard_map.86.kept_ref, ...), custom_call_target="tpu_custom_call" | custom-call | tf_op jit(solution)/shard_map/pallas_call | solution.py:336
  138.7 20.5 %shard_map.88 = (bf16[64,32,256]{2,1,0:T(8,128)(2,1)}, bf16[2,2304,256]{2,1,0:T(8,128)(2,1)}) custom-call(s32[2]{0:T(128)} %pad_add_fusion.1.steps_ref, s32[64]{0:T(128)} %add.71.refs_0_.list_ref, s32[64]{0:T(128)} %add.72.live_ref, s32[256]{0:T(256)} %reshape.77.refs_1_.geo_ref, bf16[64,4,224,256]{3,2,1,0:T(8,128)(2,1)} %shard_map.86.kept_ref, ...), custom_call_target="tpu_custom_call" | custom-call | tf_op jit(solution)/shard_map/pallas_call | solution.py:336
  159.2 64.4 %shard_map.89 = bf16[2,2304,256]{2,1,0:T(8,128)(2,1)} custom-call(bf16[2,2304,256]{2,1,0:T(8,128)(2,1)} %get-tuple-element.20.mine_ref), custom_call_target="tpu_custom_call" | custom-call | tf_op jit(solution)/shard_map/pallas_call | solution.py:498
  223.6 4.2 %fusion.5 = (f32[1,2304,256]{2,1,0:T(8,128)}, f32[1,2304,256]{2,1,0:T(8,128)}) fusion(bf16[2,2304,256]{2,1,0:T(8,128)(2,1)} %shard_map.89), kind=kLoop, calls=%fused_computation.39 | loop fusion | bytes 9437184 | tf_op jit(solution)/shard_map/slice | solution.py:586
  (18 shorter events, 0.6 us)
Async XLA Ops:
  10.2 12.3 %copy-start.2 = (s32[1,1,32,2,4,14]{2,4,5,3,1,0:T(4,128)S(1)}, s32[1,1,32,2,4,14]{2,4,5,3,1,0:T(4,128)}, u32[]{:S(2)}) copy-start(s32[1,1,32,2,4,14]{2,4,5,3,1,0:T(4,128)} %param.9) | copy-start | bytes 43012
  10.2 50.1 %all-to-all-start.1 = ((bf16[32,200,256]{2,1,0:T(8,128)(2,1)}), bf16[32,200,256]{2,1,0:T(8,128)(2,1)S(1)}, u32[]{:S(2)}, u32[]{:S(2)}) async-start(bf16[32,200,256]{2,1,0:T(8,128)(2,1)} %get-tuple-element.15), calls=%async_computation.1 | async-start | bytes 6553600 | tf_op jit(solution)/shard_map/all_to_all | solution.py:554
  60.3 1.7 copy-start
  62.0 76.7 %all-to-all-start = ((bf16[32,200,256]{2,1,0:T(8,128)(2,1)}), bf16[32,200,256]{2,1,0:T(8,128)(2,1)}, u32[]{:S(2)}, u32[]{:S(2)}) async-start(bf16[32,200,256]{2,1,0:T(8,128)(2,1)} %get-tuple-element.14), calls=%async_computation | async-start | bytes 6553600 | tf_op jit(solution)/shard_map/all_to_all | solution.py:554
  80.3 3.0 %copy-start.1 = (bf16[3,3,256,256]{3,2,1,0:T(8,128)(2,1)S(1)}, bf16[3,3,256,256]{3,2,1,0:T(8,128)(2,1)}, u32[]{:S(2)}) copy-start(bf16[3,3,256,256]{3,2,1,0:T(8,128)(2,1)} %param.11) | copy-start | bytes 3538948

commit v4 on v3

--- a/solution.py
+++ b/solution.py
@@ -121,24 +121,30 @@
     return 0.5 * jnp.tanh(0.5 * v) + 0.5
 
 
-def forward_kernel(steps_ref, *refs):
-    wide_in, wide_hid = refs[-2:]
-
-    @pl.when(pl.program_id(0) == 0)
+def forward_kernel(steps_ref, list_ref, live_ref, geo_ref, *refs):
+    first_ref, second_ref, _, turned_ref, wide_in, wide_hid = refs[1:]
+    step = pl.program_id(0)
+
+    @pl.when(step == 0)
     def _():
         clear_edges(wide_in)
         clear_edges(wide_hid)
-
-    pl.when(pl.program_id(0) < steps_ref[0])(functools.partial(forward_step, *refs))
-
-
-def forward_step(list_ref, geo_ref, tile_ref, first_ref, second_ref, out_ref, wide_in, wide_hid):
+        for w, kernel_ref in enumerate((first_ref, second_ref)):
+            for n in range(9):
+                turned_ref[w, n] = kernel_ref[8 - n].T
+
+    full = live_ref[step * PER + PER // 2] > 0
+    for per, chosen in ((PER, full), (PER // 2, jnp.logical_not(full))):
+        run = functools.partial(forward_step, per, list_ref, geo_ref, *refs)
+        pl.when((step < steps_ref[0]) & chosen)(run)
+
+
+def forward_step(per, list_ref, geo_ref, tile_ref, first_ref, second_ref, out_ref, turned_ref, wide_in, wide_hid):
     step = pl.program_id(0)
-    per = out_ref.shape[0]
     inside = (iota((FLAT, CH), 0) & 15) < RES
 
     def sample(r):
-        block = sampled_block(geo_ref, list_ref[step * per + r], tile_ref)
+        block = sampled_block(geo_ref, list_ref[step * PER + r], tile_ref)
         put_shifted(wide_in, r, block)
         out_ref[r, 0] = block.astype(BF)
 
@@ -184,26 +190,30 @@
     return jnp.minimum(step, steps_ref[0] - 1)
 
 
-def forward(steps, slots, geo, tile, first, second):
+def forward(steps, slots, live, geo, tile, first, second):
     count = slots.shape[0]
     whole = lambda *shape: pl.BlockSpec(shape, lambda i, *_: (0,) * len(shape))
     return pl.pallas_call(
         forward_kernel,
         grid_spec=pltpu.PrefetchScalarGridSpec(
-            num_scalar_prefetch=3,
+            num_scalar_prefetch=4,
             grid=(count // PER,),
             in_specs=[whole(TH, TW, CH), whole(9, CH, CH), whole(9, CH, CH)],
-            out_specs=pl.BlockSpec(
-                (PER, 4, FLAT, CH), lambda i, n, *_: (held(i, n), 0, 0, 0)
-            ),
+            out_specs=[
+                pl.BlockSpec((PER, 4, FLAT, CH), lambda i, n, *_: (held(i, n), 0, 0, 0)),
+                whole(2, 9, CH, CH),
+            ],
             scratch_shapes=[
                 pltpu.VMEM((PER, FLAT + 2 * PITCH, WIDE), BF),
                 pltpu.VMEM((PER, FLAT + 2 * PITCH, WIDE), BF),
             ],
         ),
-        out_shape=jax.ShapeDtypeStruct((count, 4, FLAT, CH), BF),
+        out_shape=[
+            jax.ShapeDtypeStruct((count, 4, FLAT, CH), BF),
+            jax.ShapeDtypeStruct((2, 9, CH, CH), BF),
+        ],
         compiler_params=pltpu.CompilerParams(vmem_limit_bytes=VMEM),
-    )(steps, slots, geo, tile, first, second)
+    )(steps, slots, live, geo, tile, first, second)
 
 
 def spread(geo_ref, slot, back, grad_ref, half):
@@ -228,9 +238,8 @@
         grad_ref[pl.ds(low, 2)] = grad_ref[pl.ds(low, 2)] + pair
 
 
-def backward_step(at, list_ref, live_ref, geo_ref, kept_ref, ups, first_ref, second_ref, scratch):
+def backward_step(per, at, list_ref, live_ref, geo_ref, kept_ref, ups, first_ref, second_ref, scratch):
     wide_two, wide_one, first_acc, second_acc, tile_acc = scratch
-    per = kept_ref.shape[0]
     unpack = (iota((FLAT, PACK), 1) == packed_place(iota((FLAT, PACK), 0))).astype(F32).astype(BF)
     def upstream(r):
         packed = jnp.where(live_ref[at + r] > 0, ups[r][0], jnp.zeros_like(ups[r][0]))
@@ -251,65 +260,78 @@
             upstream(r + 2)
         if r:
             first_delta(r - 1, held[r - 1])
-    kernel_sums(kept_ref, 1, wide_two, second_acc, 0)
+    kernel_sums(per, kept_ref, 1, wide_two, second_acc, 0)
     first_delta(per - 1, held[per - 1])
-    kernel_sums(kept_ref, 1, wide_two, second_acc, 1)
-    kernel_sums(kept_ref, 1, wide_two, second_acc, 2)
+    kernel_sums(per, kept_ref, 1, wide_two, second_acc, 1)
+    kernel_sums(per, kept_ref, 1, wide_two, second_acc, 2)
     held = []
     for r in range(per):
         held.append(conv_back(wide_one, r, first_ref).astype(BF))
     for a in range(3):
-        kernel_sums(kept_ref, 0, wide_one, first_acc, a)
-        give_back(a, held[a], 0)
-        give_back(a, held[a], 1)
-    give_back(3, held[3], 0)
-    give_back(3, held[3], 1)
-
-
-def kernel_sums(kept_ref, which, wide, acc, a):
-    per = kept_ref.shape[0]
-    values = kept_ref[:, which].reshape(per * FLAT, CH)
+        kernel_sums(per, kept_ref, 0, wide_one, first_acc, a)
+        if a < per:
+            give_back(a, held[a], 0)
+            give_back(a, held[a], 1)
+    for r in range(3, per):
+        give_back(r, held[r], 0)
+        give_back(r, held[r], 1)
+
+
+def kernel_sums(per, kept_ref, which, wide, acc, a):
+    values = kept_ref[0:per, which].reshape(per * FLAT, CH)
     acc[a] += lax.dot_general(
-        values, wide[:, PITCH * a : PITCH * a + FLAT, :].reshape(per * FLAT, WIDE),
+        values, wide[0:per, PITCH * a : PITCH * a + FLAT, :].reshape(per * FLAT, WIDE),
         (((0,), (0,)), ((), ())), preferred_element_type=F32,
     )
 
 
 def backward_kernel(begun, scale, steps_ref, list_ref, live_ref, geo_ref, kept_ref, *refs):
     ups, refs = refs[:PER], refs[PER:]
-    first_ref, second_ref, refs = refs[0], refs[1], refs[2:]
-    sums, refs = (refs[:3], refs[3:]) if begun else (None, refs)
-    scratch = refs[-5:] if begun else refs[3:5] + refs[:3]
+    turned_ref, refs = refs[0], refs[1:]
+    if begun:
+        sums, (tile_out, kernels_out), refs = refs[:3], refs[3:5], refs[5:]
+        scratch, fetched, sems = refs[:5], refs[5:8], refs[8]
+        fetches = [pltpu.make_async_copy(a, b, sems.at[n]) for n, (a, b) in enumerate(zip(sums, fetched))]
+    else:
+        scratch, fetches = refs[3:5] + refs[:3], []
     wide_two, wide_one, first_acc, second_acc, tile_acc = scratch
+    first_ref, second_ref = turned_ref.at[0], turned_ref.at[1]
     step = pl.program_id(0)
 
     @pl.when(step == 0)
     def _():
+        for fetch in fetches:
+            fetch.start()
         clear_edges(wide_two)
         clear_edges(wide_one)
         first_acc[...] = jnp.zeros_like(first_acc)
         second_acc[...] = jnp.zeros_like(second_acc)
         tile_acc[...] = jnp.zeros_like(tile_acc)
 
-    @pl.when(step < steps_ref[0])
-    def _():
-        at = (steps_ref[1] + step) * PER
-        backward_step(at, list_ref, live_ref, geo_ref, kept_ref, ups, first_ref, second_ref, scratch)
+    at = (steps_ref[1] + step) * PER
+    within = step < steps_ref[0]
+    full = live_ref[jnp.minimum(at + PER // 2, live_ref.shape[0] - 1)] > 0
+    for per, chosen in ((PER, full), (PER // 2, jnp.logical_not(full))):
+        run = functools.partial(
+            backward_step, per, at, list_ref, live_ref, geo_ref, kept_ref, ups, first_ref, second_ref, scratch
+        )
+        pl.when(within & chosen)(run)
 
     if begun:
 
         @pl.when(step == pl.num_programs(0) - 1)
         def _():
-            tile_out, kernels_out = refs[:2]
-            tile_out[...] = (tile_acc[...] + sums[2][...]).astype(BF)
+            for fetch in fetches:
+                fetch.wait()
+            tile_out[...] = (tile_acc[...] + fetched[2][...]).astype(BF)
             for n in range(9):
                 row, cols = (8 - n) // 3, slice((8 - n) % 3 * CH, ((8 - n) % 3 + 1) * CH)
                 for w, acc in enumerate((first_acc, second_acc)):
-                    total = acc[row, :, cols] + sums[w][row, :, cols]
+                    total = acc[row, :, cols] + fetched[w][row, :, cols]
                     kernels_out[w, n * CH : (n + 1) * CH] = (total * scale).astype(BF)
 
 
-def backward(slot, plan, geo, kept, arrived, first, second, sums, scale):
+def backward(slot, plan, geo, kept, arrived, turned, sums, scale):
     steps, slots, live = plan
     readers = arrived.shape[0]
     begun = sums is not None
@@ -329,7 +351,7 @@
     wide = [pltpu.VMEM((PER, FLAT + 2 * PITCH, WIDE), BF)] * 2
     if begun:
         outs = [jax.ShapeDtypeStruct((TH, TW, CH), BF), jax.ShapeDtypeStruct((2, 9 * CH, CH), BF)]
-        scratch = wide + [pltpu.VMEM(t, F32) for t in totals]
+        scratch = wide + [pltpu.VMEM(t, F32) for t in totals] * 2 + [pltpu.SemaphoreType.DMA((3,))]
     else:
         outs = [jax.ShapeDtypeStruct(t, F32) for t in totals]
         scratch = wide
@@ -341,16 +363,15 @@
             in_specs=[
                 pl.BlockSpec((PER, 4, FLAT, CH), lambda i, n, *_: (group(i, n), 0, 0, 0)),
                 *[from_reader(j) for j in range(PER)],
-                whole(9, CH, CH),
-                whole(9, CH, CH),
-                *([whole(*t) for t in totals] if begun else []),
+                whole(2, 9, CH, CH),
+                *[pl.BlockSpec(memory_space=pl.ANY)] * (3 if begun else 0),
             ],
             out_specs=[whole(*o.shape) for o in outs],
             scratch_shapes=scratch,
         ),
         out_shape=outs,
         compiler_params=pltpu.CompilerParams(vmem_limit_bytes=VMEM),
-    )(steps, slots, live, geo, kept, *[arrived] * PER, first, second, *(sums or ()))
+    )(steps, slots, live, geo, kept, *[arrived] * PER, turned, *(sums or ()))
 
 
 SIDE = 4
@@ -546,10 +567,6 @@
     return slots, live, jnp.maximum(steps_zero + steps_one, 1).reshape(1), zero, one
 
 
-def turned(kernel):
-    return jnp.transpose(kernel[::-1, ::-1], (0, 1, 3, 2)).reshape(9, CH, CH)
-
-
 def exchange(blocks):
     return lax.all_to_all(blocks, "tile", split_axis=0, concat_axis=0, tiled=True)
 
@@ -575,13 +592,12 @@
     ).reshape(-1)
     slots, live, steps, zero, one = work_plan(row)
     first, second = first_kernel.reshape(9, CH, CH), second_kernel.reshape(9, CH, CH)
-    kept = forward(steps, slots, geo, features[0], first, second)
+    kept, turned = forward(steps, slots, live, geo, features[0], first, second)
     later, kept = lax.optimization_barrier((packed[1], kept))
     arrived.append(exchange(later))
-    first, second = turned(first_kernel), turned(second_kernel)
     scale = 1.0 / math.sqrt(lines * tiles * regions * RES * RES)
-    sums = backward(0, (zero, slots, live), geo, kept, arrived[0], first, second, None, scale)
-    tile_grad, parts = backward(1, (one, slots, live), geo, kept, arrived[1], first, second, sums, scale)
+    sums = backward(0, (zero, slots, live), geo, kept, arrived[0], turned, None, scale)
+    tile_grad, parts = backward(1, (one, slots, live), geo, kept, arrived[1], turned, sums, scale)
     totals = reduce_everywhere(parts).astype(F32).reshape(2, 3, 3, CH, CH)
     return tile_grad[None], totals[0], totals[1]
 

time: 228 us -> 225 us (0.987)
  waiting for transfers between devices: 2.88 us -> 59.1 us
  Pallas kernels: 174 us -> 118 us
  local copies, waits for them, and re-layouts: 16.1 us -> 11.4 us
    all_to_all x2, waiting for transfers between devices: 2.88 us -> 59.1 us  [exchange(): lax.all_to_all(blocks, 'tile', split_axis=0, concat_axis=0, tiled=True)]
    pallas_call x2, Pallas kernels: 72.3 us -> 16.3 us  [backward(): pl.pallas_call(functools.partial(backward_kernel, begun, scale), grid_spe...]
    pallas_call x1, Pallas kernels: 33.1 us -> 8.03 us  [forward(): pl.pallas_call(forward_kernel, grid_spec=pltpu.PrefetchScalarGridSpec(num...]
    pallas_call x1, Pallas kernels: 64.4 us -> 89.1 us  [reduce_everywhere(): pl.pallas_call(reduce_kernel, in_specs=[spec], out_specs=spec, out_shape=...]
    transpose x4 -> x0, local copies, waits for them, and re-layouts: 4.65 us -> none  [turned(): return jnp.transpose(kernel[::-1, ::-1], (0, 1, 3, 2)).reshape(9, CH, CH)]
    unnamed x7 -> x5, local copies, waits for them, and re-layouts: 5.44 us -> 5.44 us
  transfers between devices with their start and end apart: 2 -> 2, of which waited for: 1 -> 2; matrix products, arithmetic and copies ran while one was open for 4% -> 2% of each run, Pallas kernels for 37% -> 7%
where the time goes in v4:
time: 225 us; the launch traced here: 224 us
  Pallas kernels  118 us (52%)
  waiting for transfers between devices  59.1 us (26%)
  starting transfers between devices  29.2 us (13%)
  local copies, waits for them, and re-layouts  11.4 us (5%)
  other arithmetic  4.81 us (2%)
    pallas_call x1, Pallas kernels, reduce_everywhere(): pl.pallas_call(reduce_kernel, in_specs=[spec], out_specs=spec, out_shape=...  89.1 us
    all_to_all x2, waiting for transfers between devices, exchange(): lax.all_to_all(blocks, 'tile', split_axis=0, concat_axis=0, tiled=True)  59.1 us
    all_to_all x2, starting transfers between devices, exchange(): lax.all_to_all(blocks, 'tile', split_axis=0, concat_axis=0, tiled=True)  29.2 us
    pallas_call x2, Pallas kernels, backward(): pl.pallas_call(functools.partial(backward_kernel, begun, scale), grid_spe...  16.3 us
    pallas_call x1, Pallas kernels, forward(): pl.pallas_call(forward_kernel, grid_spec=pltpu.PrefetchScalarGridSpec(num...  8.03 us
    unnamed x5, local copies, waits for them, and re-layouts  5.44 us
  transfers between devices with their start and end apart: 2, of which 2 were waited for; matrix products, arithmetic and copies ran while one was open for 2% of the time, Pallas kernels for 7%

profile of v4, /device:TPU:1, one launch (start us, length us, event | category | flops | bytes accessed | tf_op | source)
XLA Modules:
  0.0 224.3 jit_solution(158806860411451092)
XLA Ops:
  0.6 0.9 dynamic-slice_reduce_fusion
  1.5 0.1 select_reduce_fusion
  1.7 0.6 select_reduce_fusion.5
  2.3 3.7 %copy.17 = bf16[1,22,14,14,256]{4,3,2,1,0:T(8,128)(2,1)} copy(bf16[1,22,14,14,256]{4,1,3,2,0:T(8,128)(2,1)} %param.7) | data formatting | bytes 4415488 | tf_op args[1]
  6.0 4.2 %shard_map.85 = (bf16[32,200,256]{2,1,0:T(8,128)(2,1)}, bf16[32,200,256]{2,1,0:T(8,128)(2,1)}) custom-call(s32[22]{0:T(128)} %get-tuple-element.26.slot_ref, s32[22]{0:T(128)} %get-tuple-element.25.owner_ref, bf16[22,14,14,256]{3,2,1,0:T(8,128)(2,1)} %bitcast.25), custom_call_target="tpu_custom_call" | custom-call | tf_op jit(solution)/shard_map/pallas_call | solution.py:56
  10.3 9.6 %all-to-all-start.1 = ((bf16[32,200,256]{2,1,0:T(8,128)(2,1)}), bf16[32,200,256]{2,1,0:T(8,128)(2,1)S(1)}, u32[]{:S(2)}, u32[]{:S(2)}) async-start(bf16[32,200,256]{2,1,0:T(8,128)(2,1)} %get-tuple-element.19), calls=%async_computation.1 | async-start | bytes 6553600 | tf_op jit(solution)/shard_map/all_to_all | solution.py:571
  19.8 1.3 convert_reduce_fusion.3
  22.6 0.1 reshape.70
  22.8 0.6 reshape.71.geo_ref
  23.5 0.1 select_reduce_fusion.2
  23.6 0.1 select_reduce_fusion.4
  23.8 0.5 add.72.live_ref
  24.3 0.5 add.71.list_ref
  24.9 8.0 %shard_map.86 = (bf16[64,4,224,256]{3,2,1,0:T(8,128)(2,1)}, bf16[2,9,256,256]{3,2,1,0:T(8,128)(2,1)}) custom-call(s32[1]{0:T(128)} %bitcast.9.steps_ref, s32[64]{0:T(128)} %add.71.list_ref, s32[64]{0:T(128)} %add.72.live_ref, s32[256]{0:T(256)} %reshape.71.geo_ref, bf16[64,32,256]{2,1,0:T(8,128)(2,1)} %bitcast.30, bf16[9,256,256]{2,1,0:T(8,128)(2,1)} %bitcast.28, ...), custom_call_target="tpu_custom_call" | custom-call | tf_op jit(solution)/shard_map/pallas_call | solution.py:196
  32.9 27.5 %all-to-all-done.1.refs_0_.refs_1_.refs_2_.refs_3_ = bf16[32,200,256]{2,1,0:T(8,128)(2,1)S(1)} async-done(((bf16[32,200,256]{2,1,0:T(8,128)(2,1)}), bf16[32,200,256]{2,1,0:T(8,128)(2,1)S(1)}, u32[]{:S(2)}, u32[]{:S(2)}) %all-to-all-start.1) | async-done | bytes 3276832 | tf_op jit(solution)/shard_map/all_to_all | solution.py:571
  60.3 1.7 copy-done
  62.1 19.6 %all-to-all-start = ((bf16[32,200,256]{2,1,0:T(8,128)(2,1)}), bf16[32,200,256]{2,1,0:T(8,128)(2,1)}, u32[]{:S(2)}, u32[]{:S(2)}) async-start(bf16[32,200,256]{2,1,0:T(8,128)(2,1)} %get-tuple-element.17), calls=%async_computation | async-start | bytes 6553600 | tf_op jit(solution)/shard_map/all_to_all | solution.py:571
  81.7 0.7 pad_add_fusion.1.steps_ref
  82.4 0.6 pad_add_fusion.2.steps_ref
  83.0 7.5 %shard_map.87 = (f32[3,256,768]{2,1,0:T(8,128)}, f32[3,256,768]{2,1,0:T(8,128)}, f32[64,32,256]{2,1,0:T(8,128)}) custom-call(s32[2]{0:T(128)} %pad_add_fusion.2.steps_ref, s32[64]{0:T(128)} %add.71.list_ref, s32[64]{0:T(128)} %add.72.live_ref, s32[256]{0:T(256)} %reshape.71.geo_ref, bf16[64,4,224,256]{3,2,1,0:T(8,128)(2,1)} %get-tuple-element.16.kept_ref, ...), custom_call_target="tpu_custom_call" | custom-call | tf_op jit(solution)/shard_map/pallas_call | solution.py:358
  90.5 31.7 %all-to-all-done.refs_0_.refs_1_.refs_2_.refs_3_ = bf16[32,200,256]{2,1,0:T(8,128)(2,1)} async-done(((bf16[32,200,256]{2,1,0:T(8,128)(2,1)}), bf16[32,200,256]{2,1,0:T(8,128)(2,1)}, u32[]{:S(2)}, u32[]{:S(2)}) %all-to-all-start) | async-done | bytes 3276832 | tf_op jit(solution)/shard_map/all_to_all | solution.py:571
  122.2 8.8 %shard_map.88 = (bf16[64,32,256]{2,1,0:T(8,128)(2,1)}, bf16[2,2304,256]{2,1,0:T(8,128)(2,1)}) custom-call(s32[2]{0:T(128)} %pad_add_fusion.1.steps_ref, s32[64]{0:T(128)} %add.71.list_ref, s32[64]{0:T(128)} %add.72.live_ref, s32[256]{0:T(256)} %reshape.71.geo_ref, bf16[64,4,224,256]{3,2,1,0:T(8,128)(2,1)} %get-tuple-element.16.kept_ref, ...), custom_call_target="tpu_custom_call" | custom-call | tf_op jit(solution)/shard_map/pallas_call | solution.py:358
  131.0 89.1 %shard_map.89 = bf16[2,2304,256]{2,1,0:T(8,128)(2,1)} custom-call(bf16[2,2304,256]{2,1,0:T(8,128)(2,1)} %get-tuple-element.24.mine_ref), custom_call_target="tpu_custom_call" | custom-call | tf_op jit(solution)/shard_map/pallas_call | solution.py:519
  220.1 4.2 %fusion.5 = (f32[1,2304,256]{2,1,0:T(8,128)}, f32[1,2304,256]{2,1,0:T(8,128)}) fusion(bf16[2,2304,256]{2,1,0:T(8,128)(2,1)} %shard_map.89), kind=kLoop, calls=%fused_computation.37 | loop fusion | bytes 9437184 | tf_op jit(solution)/shard_map/slice | solution.py:602
  (12 shorter events, 0.3 us)
Async XLA Ops:
  10.3 12.3 %copy-start.1 = (s32[1,1,32,2,4,14]{2,4,5,3,1,0:T(4,128)S(1)}, s32[1,1,32,2,4,14]{2,4,5,3,1,0:T(4,128)}, u32[]{:S(2)}) copy-start(s32[1,1,32,2,4,14]{2,4,5,3,1,0:T(4,128)} %param.9) | copy-start | bytes 43012
  10.3 50.1 %all-to-all-start.1 = ((bf16[32,200,256]{2,1,0:T(8,128)(2,1)}), bf16[32,200,256]{2,1,0:T(8,128)(2,1)S(1)}, u32[]{:S(2)}, u32[]{:S(2)}) async-start(bf16[32,200,256]{2,1,0:T(8,128)(2,1)} %get-tuple-element.19), calls=%async_computation.1 | async-start | bytes 6553600 | tf_op jit(solution)/shard_map/all_to_all | solution.py:571
  60.3 1.7 copy-start
  62.1 60.1 %all-to-all-start = ((bf16[32,200,256]{2,1,0:T(8,128)(2,1)}), bf16[32,200,256]{2,1,0:T(8,128)(2,1)}, u32[]{:S(2)}, u32[]{:S(2)}) async-start(bf16[32,200,256]{2,1,0:T(8,128)(2,1)} %get-tuple-element.17), calls=%async_computation | async-start | bytes 6553600 | tf_op jit(solution)/shard_map/all_to_all | solution.py:571

commit v5 on v4

--- a/solution.py
+++ b/solution.py
@@ -144,7 +144,7 @@
     inside = (iota((FLAT, CH), 0) & 15) < RES
 
     def sample(r):
-        block = sampled_block(geo_ref, list_ref[step * PER + r], tile_ref)
+        block = sampled_block(geo_ref, slot_at(list_ref, step * PER + r), tile_ref)
         put_shifted(wide_in, r, block)
         out_ref[r, 0] = block.astype(BF)
 
@@ -184,6 +184,10 @@
 
 
 PER = 4
+
+
+def slot_at(list_ref, place):
+    return jnp.maximum(list_ref[place] - 1, 0)
 
 
 def held(step, steps_ref):
@@ -249,7 +253,7 @@
         put_shifted(wide_one, r, hidden_back * kept_ref[r, 2].astype(F32))
 
     def give_back(r, back, half):
-        spread(geo_ref, list_ref[at + r], back, tile_acc, half)
+        spread(geo_ref, slot_at(list_ref, at + r), back, tile_acc, half)
 
     upstream(0)
     upstream(1)
@@ -285,7 +289,11 @@
     )
 
 
-def backward_kernel(begun, scale, steps_ref, list_ref, live_ref, geo_ref, kept_ref, *refs):
+def base(slot, steps_ref):
+    return steps_ref[1] if slot else 0
+
+
+def backward_kernel(slot, begun, scale, steps_ref, list_ref, live_ref, geo_ref, kept_ref, *refs):
     ups, refs = refs[:PER], refs[PER:]
     turned_ref, refs = refs[0], refs[1:]
     if begun:
@@ -308,8 +316,8 @@
         second_acc[...] = jnp.zeros_like(second_acc)
         tile_acc[...] = jnp.zeros_like(tile_acc)
 
-    at = (steps_ref[1] + step) * PER
-    within = step < steps_ref[0]
+    at = (base(slot, steps_ref) + step) * PER
+    within = step < steps_ref[1 + slot]
     full = live_ref[jnp.minimum(at + PER // 2, live_ref.shape[0] - 1)] > 0
     for per, chosen in ((PER, full), (PER // 2, jnp.logical_not(full))):
         run = functools.partial(
@@ -339,11 +347,11 @@
     last = slots.shape[0] // PER - 1
 
     def group(i, n):
-        return jnp.clip(n[1] + jnp.minimum(i, n[0] - 1), 0, last)
+        return jnp.clip(base(slot, n) + jnp.minimum(i, n[1 + slot] - 1), 0, last)
 
     def from_reader(j):
         def block(i, n, s, *_):
-            return jnp.clip(s[PER * group(i, n) + j] - slot * readers, 0, readers - 1), 0, 0
+            return jnp.clip(s[PER * group(i, n) + j] - 1 - slot * readers, 0, readers - 1), 0, 0
 
         return pl.BlockSpec((1, PACK, CH), block)
 
@@ -356,7 +364,7 @@
         outs = [jax.ShapeDtypeStruct(t, F32) for t in totals]
         scratch = wide
     return pl.pallas_call(
-        functools.partial(backward_kernel, begun, scale),
+        functools.partial(backward_kernel, slot, begun, scale),
         grid_spec=pltpu.PrefetchScalarGridSpec(
             num_scalar_prefetch=4,
             grid=(readers // PER,),
@@ -449,7 +457,7 @@
         at = slice(part * third, (part + 1) * third)
         return remote(out_ref.at[of, at], out_ref.at[of, at], 3 + part, other)
 
-    shifts = range(1, SIDE)
+    shifts = (2, 1, 3)
     parts = range(3)
     for part in parts:
         swap(part).start()
@@ -479,10 +487,10 @@
             three(part, k).start()
     for part in parts:
         first, second, axis = ORDERS[part]
-        terms = [held_two[part].astype(F32)]
+        terms = {0: held_two[part].astype(F32)}
         for k in shifts:
             three(part, k).wait()
-            terms.append(in_three[part, k - 1].astype(F32))
+            terms[k] = in_three[part, k - 1].astype(F32)
         total = None
         for place in range(SIDE):
             back = (coords[axis] - place) & (SIDE - 1)
@@ -555,16 +563,13 @@
     place = jnp.arange(2 * readers, dtype=jnp.int32)[:, None]
     steps_zero = (jnp.sum(row > 0, dtype=jnp.int32) + PER - 1) // PER
     steps_one = (jnp.sum(row > 1, dtype=jnp.int32) + PER - 1) // PER
-    slots, live = 0, 0
+    slots = 0
     for s, start in ((0, 0), (1, PER * steps_zero)):
         has = row > s
         rank = jnp.sum(jnp.where((ids[None, :] < ids[:, None]) & has[None, :], 1, 0), axis=1)
         hit = has[None, :] & (start + rank[None, :] == place)
-        slots += jnp.sum(jnp.where(hit, s * readers + ids[None, :], 0), axis=1, dtype=jnp.int32)
-        live += jnp.sum(hit, axis=1, dtype=jnp.int32)
-    zero = jnp.stack([steps_zero, jnp.zeros_like(steps_zero)])
-    one = jnp.stack([steps_one, steps_zero])
-    return slots, live, jnp.maximum(steps_zero + steps_one, 1).reshape(1), zero, one
+        slots += jnp.sum(jnp.where(hit, s * readers + ids[None, :] + 1, 0), axis=1, dtype=jnp.int32)
+    return slots, jnp.stack([jnp.maximum(steps_zero + steps_one, 1), steps_zero, steps_one])
 
 
 def exchange(blocks):
@@ -590,14 +595,14 @@
         [row_at[:, 0], row_at[:, 1] - row_at[:, 0], col_at[:, 0], col_at[:, 1] - col_at[:, 0]],
         axis=1,
     ).reshape(-1)
-    slots, live, steps, zero, one = work_plan(row)
+    slots, steps = work_plan(row)
     first, second = first_kernel.reshape(9, CH, CH), second_kernel.reshape(9, CH, CH)
-    kept, turned = forward(steps, slots, live, geo, features[0], first, second)
+    kept, turned = forward(steps, slots, slots, geo, features[0], first, second)
     later, kept = lax.optimization_barrier((packed[1], kept))
     arrived.append(exchange(later))
     scale = 1.0 / math.sqrt(lines * tiles * regions * RES * RES)
-    sums = backward(0, (zero, slots, live), geo, kept, arrived[0], turned, None, scale)
-    tile_grad, parts = backward(1, (one, slots, live), geo, kept, arrived[1], turned, sums, scale)
+    sums = backward(0, (steps, slots, slots), geo, kept, arrived[0], turned, None, scale)
+    tile_grad, parts = backward(1, (steps, slots, slots), geo, kept, arrived[1], turned, sums, scale)
     totals = reduce_everywhere(parts).astype(F32).reshape(2, 3, 3, CH, CH)
     return tile_grad[None], totals[0], totals[1]
 

time: 225 us -> 222 us (0.987); the launches traced: 224 us -> 219 us
  Pallas kernels: 118 us -> 134 us
  waiting for transfers between devices: 59.1 us -> 44.7 us
  starting transfers between devices: 29.2 us -> 23.4 us
    all_to_all x2, waiting for transfers between devices: 59.1 us -> 44.7 us  [exchange(): lax.all_to_all(blocks, 'tile', split_axis=0, concat_axis=0, tiled=True)]
    pallas_call x2, Pallas kernels: 16.3 us -> 27.4 us  [backward(): pl.pallas_call(functools.partial(backward_kernel, slot, begun, scale), gr...]
    all_to_all x2, starting transfers between devices: 29.2 us -> 23.4 us  [exchange(): lax.all_to_all(blocks, 'tile', split_axis=0, concat_axis=0, tiled=True)]
    pallas_call x1, Pallas kernels: 8.03 us -> 12 us  [forward(): pl.pallas_call(forward_kernel, grid_spec=pltpu.PrefetchScalarGridSpec(num...]
  transfers between devices with their start and end apart: 2 -> 2, of which waited for: 2 -> 2; matrix products, arithmetic and copies ran while one was open for 2% -> 2% of each run, Pallas kernels for 7% -> 14%
where the time goes in v5:
time: 222 us; the launch traced here: 219 us
  Pallas kernels  134 us (60%)
  waiting for transfers between devices  44.7 us (20%)
  starting transfers between devices  23.4 us (11%)
  local copies, waits for them, and re-layouts  11.4 us (5%)
  other arithmetic  3.59 us (2%)
    pallas_call x1, Pallas kernels, reduce_everywhere(): pl.pallas_call(reduce_kernel, in_specs=[spec], out_specs=spec, out_shape=...  89.9 us
    all_to_all x2, waiting for transfers between devices, exchange(): lax.all_to_all(blocks, 'tile', split_axis=0, concat_axis=0, tiled=True)  44.7 us
    pallas_call x2, Pallas kernels, backward(): pl.pallas_call(functools.partial(backward_kernel, slot, begun, scale), gr...  27.4 us
    all_to_all x2, starting transfers between devices, exchange(): lax.all_to_all(blocks, 'tile', split_axis=0, concat_axis=0, tiled=True)  23.4 us
    pallas_call x1, Pallas kernels, forward(): pl.pallas_call(forward_kernel, grid_spec=pltpu.PrefetchScalarGridSpec(num...  12 us
    unnamed x5, local copies, waits for them, and re-layouts  5.44 us
  transfers between devices with their start and end apart: 2, of which 2 were waited for; matrix products, arithmetic and copies ran while one was open for 2% of the time, Pallas kernels for 14%

profile of v5, /device:TPU:1, one launch (start us, length us, event | category | flops | bytes accessed | tf_op | source)
XLA Modules:
  0.0 218.8 jit_solution(1147961845518187149)
XLA Ops:
  0.6 0.9 dynamic-slice_reduce_fusion
  1.5 0.1 select_reduce_fusion
  1.7 0.6 select_reduce_fusion.5
  2.3 3.7 %copy.17 = bf16[1,22,14,14,256]{4,3,2,1,0:T(8,128)(2,1)} copy(bf16[1,22,14,14,256]{4,1,3,2,0:T(8,128)(2,1)} %param.7) | data formatting | bytes 4415488 | tf_op args[1]
  6.0 4.2 %shard_map.85 = (bf16[32,200,256]{2,1,0:T(8,128)(2,1)}, bf16[32,200,256]{2,1,0:T(8,128)(2,1)}) custom-call(s32[22]{0:T(128)} %get-tuple-element.26.slot_ref, s32[22]{0:T(128)} %get-tuple-element.25.owner_ref, bf16[22,14,14,256]{3,2,1,0:T(8,128)(2,1)} %bitcast.25), custom_call_target="tpu_custom_call" | custom-call | tf_op jit(solution)/shard_map/pallas_call | solution.py:56
  10.3 9.6 %all-to-all-start.1 = ((bf16[32,200,256]{2,1,0:T(8,128)(2,1)}), bf16[32,200,256]{2,1,0:T(8,128)(2,1)S(1)}, u32[]{:S(2)}, u32[]{:S(2)}) async-start(bf16[32,200,256]{2,1,0:T(8,128)(2,1)} %get-tuple-element.19), calls=%async_computation.1 | async-start | bytes 6553600 | tf_op jit(solution)/shard_map/all_to_all | solution.py:576
  19.9 1.3 convert_reduce_fusion.1
  22.6 0.1 reshape.72
  22.7 0.1 copy.14
  22.8 0.6 reshape.73.geo_ref
  23.5 0.1 select_reduce_fusion.4
  23.6 0.1 select_reduce_fusion.2
  23.7 0.1 select_reduce_fusion.1
  23.8 0.5 add.81.list_ref.live_ref
  24.4 0.6 pad_add_fusion.1.steps_ref
  25.0 12.0 %shard_map.86 = (bf16[64,4,224,256]{3,2,1,0:T(8,128)(2,1)}, bf16[2,9,256,256]{3,2,1,0:T(8,128)(2,1)}) custom-call(s32[3]{0:T(128)} %pad_add_fusion.1.steps_ref, s32[64]{0:T(128)} %add.81.list_ref.live_ref, s32[64]{0:T(128)} %add.81.list_ref.live_ref, s32[256]{0:T(256)} %reshape.73.geo_ref, bf16[64,32,256]{2,1,0:T(8,128)(2,1)} %bitcast.30, ...), custom_call_target="tpu_custom_call" | custom-call | tf_op jit(solution)/shard_map/pallas_call | solution.py:200
  37.0 23.4 %all-to-all-done.1.refs_0_.refs_1_.refs_2_.refs_3_ = bf16[32,200,256]{2,1,0:T(8,128)(2,1)S(1)} async-done(((bf16[32,200,256]{2,1,0:T(8,128)(2,1)}), bf16[32,200,256]{2,1,0:T(8,128)(2,1)S(1)}, u32[]{:S(2)}, u32[]{:S(2)}) %all-to-all-start.1) | async-done | bytes 3276832 | tf_op jit(solution)/shard_map/all_to_all | solution.py:576
  60.4 1.7 copy-done
  62.1 13.8 %all-to-all-start = ((bf16[32,200,256]{2,1,0:T(8,128)(2,1)}), bf16[32,200,256]{2,1,0:T(8,128)(2,1)}, u32[]{:S(2)}, u32[]{:S(2)}) async-start(bf16[32,200,256]{2,1,0:T(8,128)(2,1)} %get-tuple-element.17), calls=%async_computation | async-start | bytes 6553600 | tf_op jit(solution)/shard_map/all_to_all | solution.py:576
  75.9 18.6 %shard_map.87 = (f32[3,256,768]{2,1,0:T(8,128)}, f32[3,256,768]{2,1,0:T(8,128)}, f32[64,32,256]{2,1,0:T(8,128)}) custom-call(s32[3]{0:T(128)} %pad_add_fusion.1.steps_ref, s32[64]{0:T(128)} %add.81.list_ref.live_ref, s32[64]{0:T(128)} %add.81.list_ref.live_ref, s32[256]{0:T(256)} %reshape.73.geo_ref, bf16[64,4,224,256]{3,2,1,0:T(8,128)(2,1)} %get-tuple-element.16.kept_ref, ...), custom_call_target="tpu_custom_call" | custom-call | tf_op jit(solution)/shard_map/pallas_call | solution.py:366
  94.6 21.3 %all-to-all-done.refs_0_.refs_1_.refs_2_.refs_3_ = bf16[32,200,256]{2,1,0:T(8,128)(2,1)} async-done(((bf16[32,200,256]{2,1,0:T(8,128)(2,1)}), bf16[32,200,256]{2,1,0:T(8,128)(2,1)}, u32[]{:S(2)}, u32[]{:S(2)}) %all-to-all-start) | async-done | bytes 3276832 | tf_op jit(solution)/shard_map/all_to_all | solution.py:576
  115.9 8.8 %shard_map.88 = (bf16[64,32,256]{2,1,0:T(8,128)(2,1)}, bf16[2,2304,256]{2,1,0:T(8,128)(2,1)}) custom-call(s32[3]{0:T(128)} %pad_add_fusion.1.steps_ref, s32[64]{0:T(128)} %add.81.list_ref.live_ref, s32[64]{0:T(128)} %add.81.list_ref.live_ref, s32[256]{0:T(256)} %reshape.73.geo_ref, bf16[64,4,224,256]{3,2,1,0:T(8,128)(2,1)} %get-tuple-element.16.kept_ref, ...), custom_call_target="tpu_custom_call" | custom-call | tf_op jit(solution)/shard_map/pallas_call | solution.py:366
  124.7 89.9 %shard_map.89 = bf16[2,2304,256]{2,1,0:T(8,128)(2,1)} custom-call(bf16[2,2304,256]{2,1,0:T(8,128)(2,1)} %get-tuple-element.24.mine_ref), custom_call_target="tpu_custom_call" | custom-call | tf_op jit(solution)/shard_map/pallas_call | solution.py:527
  214.6 4.2 %fusion.5 = (f32[1,2304,256]{2,1,0:T(8,128)}, f32[1,2304,256]{2,1,0:T(8,128)}) fusion(bf16[2,2304,256]{2,1,0:T(8,128)(2,1)} %shard_map.89), kind=kLoop, calls=%fused_computation.35 | loop fusion | bytes 9437184 | tf_op jit(solution)/shard_map/slice | solution.py:607
  (11 shorter events, 0.1 us)
Async XLA Ops:
  10.3 12.3 %copy-start.1 = (s32[1,1,32,2,4,14]{2,4,5,3,1,0:T(4,128)S(1)}, s32[1,1,32,2,4,14]{2,4,5,3,1,0:T(4,128)}, u32[]{:S(2)}) copy-start(s32[1,1,32,2,4,14]{2,4,5,3,1,0:T(4,128)} %param.9) | copy-start | bytes 43012
  10.3 50.1 %all-to-all-start.1 = ((bf16[32,200,256]{2,1,0:T(8,128)(2,1)}), bf16[32,200,256]{2,1,0:T(8,128)(2,1)S(1)}, u32[]{:S(2)}, u32[]{:S(2)}) async-start(bf16[32,200,256]{2,1,0:T(8,128)(2,1)} %get-tuple-element.19), calls=%async_computation.1 | async-start | bytes 6553600 | tf_op jit(solution)/shard_map/all_to_all | solution.py:576
  60.4 1.7 copy-start
  62.1 53.8 %all-to-all-start = ((bf16[32,200,256]{2,1,0:T(8,128)(2,1)}), bf16[32,200,256]{2,1,0:T(8,128)(2,1)}, u32[]{:S(2)}, u32[]{:S(2)}) async-start(bf16[32,200,256]{2,1,0:T(8,128)(2,1)} %get-tuple-element.17), calls=%async_computation | async-start | bytes 6553600 | tf_op jit(solution)/shard_map/all_to_all | solution.py:576
